TPU v7x, 32 devices: a whole 2x2x4 slice. The times are simulated.
32 devices in a mesh: fsdp: 8 (over y, x, core), tensor: 4 (over z).
Axes of the slice: x: 2, y: 2, z: 4, core: 2. Of those that a mesh axis runs over, the one named last changes fastest.
Arguments:
- momentum: bfloat16 [3, 2, 4096, 1536], P(None, None, 'fsdp', 'tensor'), may hold values from -6 to 6
- gradient: bfloat16 [3, 2, 4096, 1536], P(None, None, 'fsdp', 'tensor'), may hold values from -4.2 to 4.2
- right_in: bfloat16 [3, 2, 1536, 128], P(None, None, 'tensor'), may hold values from -6 to 6
- owners: int32 [3], replicated, may hold values from 0 to 3, as said below
Outputs:
- state_out: bfloat16 [8, 2, 4096, 1536], P('tensor', None, 'fsdp')
- left_out: float32 [8, 2, 4096, 128], P('tensor', None, 'fsdp')
- right_out: float32 [3, 2, 1536, 128], P(None, None, 'tensor')
Inputs may be any that keep to these rules, and one draw needn't show every extreme that they name: `owners`: each entry is a tensor index. No tensor index takes more than 2 experts, and some index takes exactly 2.
All inputs are finite; a program needn't handle non-finite values.
Results may differ from a plain program's by a relative error of at most 0.0072.
Values may be sent and summed in bfloat16 or wider, within the bound.
A program may use at most 64 MiB of HBM per device.

v0:
```python
import math

import jax
import jax.numpy as jnp
from jax import lax
from jax.sharding import PartitionSpec as P

D = 4096
CAP = 2


ridge_term = 0.001
feedback = 0.1
epsilon = 1e-06


def orthonormal(panel, gram_total):
    eye_matrix = jnp.eye(gram_total.shape[-1], dtype=jnp.float32)
    lower_factor = jnp.linalg.cholesky(gram_total + ridge_term * eye_matrix)
    solved = jax.scipy.linalg.solve_triangular(
        lower_factor, jnp.swapaxes(panel, -1, -2), lower=True
    )
    return jnp.swapaxes(solved, -1, -2)


def slot_table(owners, groups, capacity):
    count = owners.shape[0]
    index_line = jnp.arange(count, dtype=jnp.int32)
    same_owner = owners[:, None] == owners[None, :]
    earlier = index_line[None, :] < index_line[:, None]
    position = jnp.sum((same_owner & earlier).astype(jnp.int32), axis=1)
    owner_hit = owners[:, None, None] == jnp.arange(groups, dtype=jnp.int32)[None, :, None]
    slot_hit = position[:, None, None] == jnp.arange(capacity, dtype=jnp.int32)[None, None, :]
    return (owner_hit & slot_hit).astype(jnp.float32)


def shards(momentum, gradient, right_in, owners):
    highest = lax.Precision.HIGHEST
    groups = lax.axis_size("tensor")
    rows = momentum.shape[2]
    columns = momentum.shape[3]
    owner_table = slot_table(owners, groups, CAP)
    table_low = owner_table.astype(jnp.bfloat16)
    summed = (momentum.astype(jnp.float32) + gradient.astype(jnp.float32)).astype(jnp.bfloat16)
    scale = math.sqrt(D)
    send_state = jnp.einsum(
        "edc,emrk->cmrdk", table_low, summed, preferred_element_type=jnp.float32
    ).astype(jnp.bfloat16)
    send_right = jnp.einsum(
        "edc,emkq->cmkdq", table_low, right_in, preferred_element_type=jnp.float32
    ).astype(jnp.bfloat16)
    got_state, got_right = (
        lax.all_to_all(send_state, "tensor", split_axis=3, concat_axis=3, tiled=True),
        lax.all_to_all(send_right, "tensor", split_axis=3, concat_axis=3, tiled=True),
    )
    panel = jnp.einsum(
        "cmrtk,cmktq->cmrq", got_state, got_right, preferred_element_type=jnp.float32
    )
    gram_part = jnp.einsum("cmrq,cmrs->cmqs", panel, panel, precision=highest)
    gram_total = lax.psum(gram_part, "fsdp")
    ortho = orthonormal(panel, gram_total)
    ortho_low = ortho.astype(jnp.bfloat16)
    factor_part = jnp.einsum(
        "cmrtk,cmrq->cmktq", got_state, ortho_low, preferred_element_type=jnp.float32
    )
    factor = lax.psum(factor_part, "fsdp")
    mean_square = jnp.mean(factor * factor, axis=(2, 3))
    right_new = factor * lax.rsqrt(mean_square + epsilon)[:, :, None, None, :]
    update = jnp.einsum("cmrq,cmktq->cmrtk", ortho, factor, precision=highest)
    fresh = (got_state.astype(jnp.float32) - feedback * update).astype(jnp.bfloat16)
    state_out = fresh.reshape(CAP, fresh.shape[1], rows, groups * columns)
    left_out = ortho * scale
    returned = lax.all_to_all(right_new, "tensor", split_axis=3, concat_axis=3, tiled=True)
    right_out = jnp.einsum("edc,cmkdq->emkq", owner_table, returned, precision=highest)
    return (state_out, left_out, right_out)


def solution(mesh):
    return jax.shard_map(
        shards,
        mesh=mesh,
        in_specs=(
            P(None, None, "fsdp", "tensor"),
            P(None, None, "fsdp", "tensor"),
            P(None, None, "tensor", None),
            P(),
        ),
        out_specs=(
            P("tensor", None, "fsdp", None),
            P("tensor", None, "fsdp", None),
            P(None, None, "tensor", None),
        ),
        check_vma=False,
    )
```

profile of v0, /device:TPU:0, one launch (start us, length us, event | category | flops | bytes accessed | tf_op | source)
XLA Modules:
  0.0 529.7 jit_solution(17150008540267646072)
XLA Ops:
  8.8 3.0 fusion.2
  11.8 3.9 convert_bitcast_fusion
  15.6 7.6 %copy.42 = bf16[2,2,512,4,384]{4,0,2,1,3:T(2,128)(2,1)} copy(bf16[2,2,512,4,384]{4,3,0,2,1:T(4,128)(2,1)S(1)} %convert_bitcast_fusion) | data formatting | bytes 12582912 | tf_op jit(solution)/shard_map/convert_element_type | solution.py:48
  23.2 6.4 %all-to-all-start = ((bf16[2,2,512,4,384]{4,0,2,1,3:T(2,128)(2,1)}), bf16[2,2,512,4,384]{4,0,2,1,3:T(2,128)(2,1)}, u32[]{:S(2)}, u32[]{:S(2)}) async-start(bf16[2,2,512,4,384]{4,0,2,1,3:T(2,128)(2,1)} %copy.42), calls=%async_computation | async-start | bytes 12582912 | tf_op jit(solution)/shard_map/all_to_all | solution.py:53
  29.7 1.4 fusion.5
  31.1 1.5 copy.46
  32.5 135.9 %all-to-all-done = bf16[2,2,512,4,384]{4,0,2,1,3:T(2,128)(2,1)} async-done(((bf16[2,2,512,4,384]{4,0,2,1,3:T(2,128)(2,1)}), bf16[2,2,512,4,384]{4,0,2,1,3:T(2,128)(2,1)}, u32[]{:S(2)}, u32[]{:S(2)}) %all-to-all-start) | async-done | bytes 6291488 | tf_op jit(solution)/shard_map/all_to_all | solution.py:53
  168.4 3.6 all-to-all-start.1
  172.0 16.1 %copy.43 = bf16[2,2,512,4,384]{2,4,3,1,0:T(8,128)(2,1)} copy(bf16[2,2,512,4,384]{4,0,2,1,3:T(2,128)(2,1)} %all-to-all-done) | data formatting | bytes 12582912 | tf_op jit(solution)/shard_map/all_to_all | solution.py:53
  188.1 20.5 %all-to-all-done.1 = bf16[2,2,384,4,128]{4,2,1,0,3:T(8,128)(2,1)S(1)} async-done(((bf16[2,2,384,4,128]{4,2,1,0,3:T(8,128)(2,1)}), bf16[2,2,384,4,128]{4,2,1,0,3:T(8,128)(2,1)S(1)}, u32[]{:S(2)}, u32[]{:S(2)}) %all-to-all-start.1) | async-done | bytes 1572896 | tf_op jit(solution)/shard_map/all_to_all | solution.py:54
  208.6 5.0 fusion.6
  213.6 2.5 fusion.29
  216.6 52.3 %all-reduce.3.cloned.1.call-done = f32[2,2,128,128]{2,3,1,0:T(8,128)} async-done(((f32[2,2,128,128]{2,3,1,0:T(8,128)}), f32[2,2,128,128]{2,3,1,0:T(8,128)}) %all-reduce.3.cloned.1.call-update) | async-done | bytes 262160 | tf_op jit(solution)/shard_map/psum | solution.py:60
  268.8 1.0 broadcast_add_fusion
  269.9 1.0 fusion.16
  270.9 46.9 %custom-call.8 = f32[2,2,128,128]{3,2,1,0:T(8,128)S(1)} custom-call(f32[2,2,128,128]{3,2,1,0:T(8,128)S(1)} %fusion.16), custom_call_target="Cholesky" | custom-call | tf_op jit(solution)/shard_map/jit(cholesky)/cholesky | solution.py:19
  318.1 39.3 %custom-call.9 = f32[2,2,1,128,128]{3,4,2,1,0:T(8,128)S(1)} custom-call(f32[2,2,1,128,128]{4,3,2,1,0:T(8,128)S(1)} %select_bitcast_fusion), custom_call_target="InvertDiagBlocksLowerTriangular" | custom-call | tf_op jit(solution)/shard_map/jit(_solve_triangular)/vmap(vmap())/triangular_solve | solution.py:20
  357.5 1.1 fusion.14
  358.6 1.0 copy-done.1
  359.5 6.6 %convolution_bitcast_fusion = f32[2,2,384,4,128]{2,4,3,1,0:T(8,128)} fusion(bf16[2,2,512,4,384]{2,4,3,1,0:T(8,128)(2,1)} %copy.43, f32[2,2,128,512]{3,2,1,0:T(8,128)S(1)} %fusion.14), kind=kOutput, calls=%fused_computation.7 | convolution fusion | flops 805568512 | bytes 10485760 | tf_op jit(solution)/shard_map/cmrtk,cmrq->cmktq/dot_general | solution.py:63
  366.2 69.0 %all-reduce.5.cloned.1.call-done = f32[2,2,384,4,128]{2,4,3,1,0:T(8,128)} async-done(((f32[2,2,384,4,128]{2,4,3,1,0:T(8,128)}), f32[2,2,384,4,128]{2,4,3,1,0:T(8,128)}) %all-reduce.5.cloned.1.call-update) | async-done | bytes 3145744 | tf_op jit(solution)/shard_map/psum | solution.py:66
  435.2 2.3 multiply_reduce_fusion
  438.3 1.9 copy.56
  440.2 4.9 all-to-all-start.2
  445.1 2.3 multiply_bitcast_fusion
  447.4 2.5 copy.59
  449.9 14.4 %fusion = bf16[2,2,512,4,384]{2,4,3,1,0:T(8,128)(2,1)} fusion(bf16[2,2,512,4,384]{2,4,3,1,0:T(8,128)(2,1)} %copy.43, f32[2,2,384,4,128]{2,4,3,1,0:T(8,128)S(1)} %copy-done, f32[2,2,128,512]{3,2,1,0:T(8,128)} %copy-done.1), kind=kOutput, calls=%fused_computation.1 | convolution fusion | flops 4844421120 | bytes 16777216 | tf_op jit(solution)/shard_map/cmrq,cmktq->cmrtk/dot_general | solution.py:69
  464.3 8.6 %copy.58 = bf16[2,2,512,1536]{3,2,1,0:T(8,128)(2,1)} copy(bf16[2,2,512,1536]{2,3,1,0:T(8,128)(2,1)} %bitcast.63) | data formatting | bytes 12582912
  472.9 42.7 %all-to-all-done.2 = f32[2,2,384,4,128]{2,4,1,0,3:T(8,128)} async-done(((f32[2,2,384,4,128]{2,4,1,0,3:T(8,128)}), f32[2,2,384,4,128]{2,4,1,0,3:T(8,128)}, u32[]{:S(2)}, u32[]{:S(2)}) %all-to-all-start.2) | async-done | bytes 3145760 | tf_op jit(solution)/shard_map/all_to_all | solution.py:73
  515.7 3.4 copy.57
  519.1 2.8 convolution_bitcast_fusion.1
  521.8 1.1 copy.60
  (22 shorter events, 3.3 us)
Async XLA Ops:
  23.2 6.5 %copy-start.2 = (bf16[3,2,384,128]{3,2,1,0:T(8,128)(2,1)S(1)}, bf16[3,2,384,128]{3,2,1,0:T(8,128)(2,1)}, u32[]{:S(2)}) copy-start(bf16[3,2,384,128]{3,2,1,0:T(8,128)(2,1)} %param.6) | copy-start | bytes 1769476
  23.2 145.2 %all-to-all-start = ((bf16[2,2,512,4,384]{4,0,2,1,3:T(2,128)(2,1)}), bf16[2,2,512,4,384]{4,0,2,1,3:T(2,128)(2,1)}, u32[]{:S(2)}, u32[]{:S(2)}) async-start(bf16[2,2,512,4,384]{4,0,2,1,3:T(2,128)(2,1)} %copy.42), calls=%async_computation | async-start | bytes 12582912 | tf_op jit(solution)/shard_map/all_to_all | solution.py:53
  168.4 40.2 %all-to-all-start.1 = ((bf16[2,2,384,4,128]{4,2,1,0,3:T(8,128)(2,1)}), bf16[2,2,384,4,128]{4,2,1,0,3:T(8,128)(2,1)S(1)}, u32[]{:S(2)}, u32[]{:S(2)}) async-start(bf16[2,2,384,4,128]{4,2,1,0,3:T(8,128)(2,1)} %copy.46), calls=%async_computation.1 | async-start | bytes 3145728 | tf_op jit(solution)/shard_map/all_to_all | solution.py:54
  172.0 96.9 %all-reduce.3.cloned.1.call-start = ((), (), s32[]{:S(2)}) async-start(), calls=%async_computation.3 | async-start | bytes 524288 | tf_op jit(solution)/shard_map/psum | solution.py:60
  216.2 219.0 %all-reduce.5.cloned.1.call-start = ((), (), s32[]{:S(2)}) async-start(), calls=%async_computation.4 | async-start | bytes 6291456 | tf_op jit(solution)/shard_map/psum | solution.py:66
  358.5 1.0 copy-start.1
  435.2 2.8 copy-start
  440.2 75.5 %all-to-all-start.2 = ((f32[2,2,384,4,128]{2,4,1,0,3:T(8,128)}), f32[2,2,384,4,128]{2,4,1,0,3:T(8,128)}, u32[]{:S(2)}, u32[]{:S(2)}) async-start(f32[2,2,384,4,128]{2,4,1,0,3:T(8,128)} %copy.56), calls=%async_computation.2 | async-start | bytes 6291456 | tf_op jit(solution)/shard_map/all_to_all | solution.py:73
Sparse Core Ops, SparseCore 0:
  216.3 52.4 all-reduce.2
  366.3 68.8 all-reduce.4
where the time goes:
time: 531 us; the launch traced here: 530 us
  waiting for transfers between devices  320 us (60%)
  other arithmetic  98.1 us (18%)
  local copies, waits for them, and re-layouts  44.3 us (8%)
  matrix products  37.6 us (7%)
  starting transfers between devices  15.1 us (3%)
  between operations  14.2 us (3%)
    all_to_all x1, waiting for transfers between devices, shards(): lax.all_to_all(send_state, 'tensor', split_axis=3, concat_axis=3, tiled=T...  136 us
    psum x1, waiting for transfers between devices, shards(): factor = lax.psum(factor_part, 'fsdp')  69 us
    psum x1, waiting for transfers between devices, shards(): gram_total = lax.psum(gram_part, 'fsdp')  52.3 us
    another operation x4, other arithmetic, orthonormal(): lower_factor = jnp.linalg.cholesky(gram_total + ridge_term * eye_matrix)  47.1 us
    all_to_all x1, waiting for transfers between devices, shards(): lax.all_to_all(right_new, 'tensor', split_axis=3, concat_axis=3, tiled=True)  42.7 us
    another operation x3, other arithmetic, orthonormal(): jax.scipy.linalg.solve_triangular(lower_factor, jnp.swapaxes(panel, -1, -...  39.5 us
    all_to_all x1, waiting for transfers between devices, shards(): lax.all_to_all(send_right, 'tensor', split_axis=3, concat_axis=3, tiled=T...  20.5 us
    all_to_all x1, local copies, waits for them, and re-layouts, shards(): lax.all_to_all(send_state, 'tensor', split_axis=3, concat_axis=3, tiled=T...  16.1 us
  transfers between devices with their start and end apart: 5, of which 5 were waited for; matrix products, arithmetic and copies ran while one was open for 9% of the time, Pallas kernels for 0%

commit v1 on v0

--- a/solution.py
+++ b/solution.py
@@ -1,8 +1,11 @@
+import functools
 import math
 
 import jax
 import jax.numpy as jnp
 from jax import lax
+from jax.experimental import pallas as pl
+from jax.experimental.pallas import tpu as pltpu
 from jax.sharding import PartitionSpec as P
 
 D = 4096
@@ -34,7 +37,7 @@
     return (owner_hit & slot_hit).astype(jnp.float32)
 
 
-def shards(momentum, gradient, right_in, owners):
+def general_shards(momentum, gradient, right_in, owners):
     highest = lax.Precision.HIGHEST
     groups = lax.axis_size("tensor")
     rows = momentum.shape[2]
@@ -75,9 +78,435 @@
     return (state_out, left_out, right_out)
 
 
+MESH = pl.DeviceIdType.MESH
+HIGHEST = lax.Precision.HIGHEST
+VMEM_BYTES = 56 * 1024 * 1024
+
+
+def greet(shards_f, groups):
+    f = lax.axis_index("fsdp")
+    z = lax.axis_index("tensor")
+    barrier = pltpu.get_barrier_semaphore()
+    for j in range(1, shards_f):
+        pl.semaphore_signal(
+            barrier, inc=1, device_id={"fsdp": lax.rem(f + j, shards_f), "tensor": z}, device_id_type=MESH
+        )
+    for j in range(1, groups):
+        pl.semaphore_signal(
+            barrier, inc=1, device_id={"fsdp": f, "tensor": lax.rem(z + j, groups)}, device_id_type=MESH
+        )
+    pl.semaphore_wait(barrier, shards_f - 1 + groups - 1)
+    return f, z
+
+
+def remote(src, dst, send_sem, recv_sem, f, z):
+    return pltpu.make_async_remote_copy(
+        src_ref=src,
+        dst_ref=dst,
+        send_sem=send_sem,
+        recv_sem=recv_sem,
+        device_id={"fsdp": f, "tensor": z},
+        device_id_type=MESH,
+    )
+
+
+def exchange_kernel(
+    shards_f, groups, kinds,
+    sel_ref, m_ref, g_ref, r_ref,
+    got_out, panel_ref, gram_ref,
+    sendbuf, got, rfull, gpart, gpair, ghalf, gfour, gfin,
+    s_send, s_recv, rz_send, rz_recv, rf_send, rf_recv, g_send, g_recv, out_sem,
+):
+    rows, columns = m_ref.shape[2], m_ref.shape[3]
+    piece = columns // shards_f
+    f, z = greet(shards_f, groups)
+    mine = pl.ds(pl.multiple_of(f * piece, piece), piece)
+
+    rfull[z, :, mine, :] = r_ref[:, mine, :]
+    right_z = []
+    for j in range(1, groups):
+        part = rfull.at[z, :, mine, :]
+        copy = remote(part, part, rz_send.at[j - 1], rz_recv.at[j - 1], f, lax.rem(z + j, groups))
+        copy.start()
+        right_z.append(copy)
+
+    step = 128
+    here = pl.ds(pl.multiple_of(z * columns, columns), columns)
+    sends = []
+    for j in (2, 3, 1):
+        d = lax.rem(z + j, groups)
+        for c in range(CAP):
+            expert = sel_ref[d * CAP + c]
+            slot = (j - 1) * CAP + c
+            for k in range(kinds):
+                @pl.loop(0, rows // step)
+                def _(i):
+                    at = pl.ds(pl.multiple_of(i * step, step), step)
+                    total = m_ref[expert, k, at, :].astype(jnp.float32) + g_ref[expert, k, at, :].astype(jnp.float32)
+                    sendbuf[slot, k, at, :] = total.astype(jnp.bfloat16)
+            copy = remote(
+                sendbuf.at[slot],
+                got.at[pl.ds(c * kinds, kinds), :, here],
+                s_send.at[slot],
+                s_recv.at[slot],
+                f,
+                d,
+            )
+            copy.start()
+            sends.append(copy)
+    for c in range(CAP):
+        expert = sel_ref[z * CAP + c]
+        for k in range(kinds):
+            @pl.loop(0, rows // step)
+            def _(i):
+                at = pl.ds(pl.multiple_of(i * step, step), step)
+                total = m_ref[expert, k, at, :].astype(jnp.float32) + g_ref[expert, k, at, :].astype(jnp.float32)
+                got[c * kinds + k, at, here] = total.astype(jnp.bfloat16)
+
+    for j in range(1, groups):
+        part = rfull.at[lax.rem(z + groups - j, groups), :, mine, :]
+        remote(part, part, rz_send.at[j - 1], rz_recv.at[j - 1], f, z).wait_recv()
+    right_f = []
+    for j in range(1, shards_f):
+        part = rfull.at[:, :, mine, :]
+        copy = remote(part, part, rf_send.at[j - 1], rf_recv.at[j - 1], lax.rem(f + j, shards_f), z)
+        copy.start()
+        right_f.append(copy)
+    for j in range(1, shards_f):
+        theirs = pl.ds(pl.multiple_of(lax.rem(f + shards_f - j, shards_f) * piece, piece), piece)
+        part = rfull.at[:, :, theirs, :]
+        remote(part, part, rf_send.at[j - 1], rf_recv.at[j - 1], f, z).wait_recv()
+
+    outs = []
+    order = (0, 1, 2, 3)
+    for j in order:
+        source = lax.rem(z + groups - j, groups)
+        there = pl.ds(pl.multiple_of(source * columns, columns), columns)
+        for c in range(CAP):
+            slot = (j - 1) * CAP + c
+            block = got.at[pl.ds(c * kinds, kinds), :, there]
+            if j:
+                remote(sendbuf.at[slot], block, s_send.at[slot], s_recv.at[slot], f, z).wait_recv()
+            copy = pltpu.make_async_copy(
+                block, got_out.at[pl.ds(c * kinds, kinds), :, there], out_sem.at[j * CAP + c]
+            )
+            copy.start()
+            outs.append(copy)
+            expert = sel_ref[z * CAP + c]
+            for k in range(kinds):
+                term = jnp.dot(
+                    got[c * kinds + k, :, there],
+                    rfull[source, expert * kinds + k],
+                    preferred_element_type=jnp.float32,
+                )
+                if j:
+                    panel_ref[c * kinds + k] += term
+                else:
+                    panel_ref[c * kinds + k] = term
+
+    mats = CAP * kinds
+    half = mats // 2
+    core = lax.rem(f, 2)
+    chip = f // 2
+    chips = shards_f // 2
+    pair = chip * 2 + 1 - core
+    for m in range(mats):
+        panel = panel_ref[m]
+        gpart[m] = jnp.dot(panel.T, panel, precision=HIGHEST, preferred_element_type=jnp.float32)
+    first = remote(gpart.at[pl.ds((1 - core) * half, half)], gpair, g_send.at[0], g_recv.at[0], pair, z)
+    first.start()
+    first.wait_recv()
+    ghalf[...] = gpart[pl.ds(core * half, half)] + gpair[...]
+    second = []
+    for j in range(1, chips):
+        copy = remote(
+            ghalf, gfour.at[j - 1], g_send.at[j], g_recv.at[j], lax.rem(chip + j, chips) * 2 + core, z
+        )
+        copy.start()
+        second.append(copy)
+    for copy in second:
+        copy.wait_recv()
+    total = ghalf[...]
+    for j in range(1, chips):
+        total = total + gfour[j - 1]
+    gfin[pl.ds(core * half, half)] = total
+    part = gfin.at[pl.ds(core * half, half)]
+    third = remote(part, part, g_send.at[chips], g_recv.at[chips], pair, z)
+    third.start()
+    part = gfin.at[pl.ds((1 - core) * half, half)]
+    remote(part, part, g_send.at[chips], g_recv.at[chips], pair, z).wait_recv()
+    gram_ref[...] = gfin[...]
+
+    for copy in right_z + sends + right_f + [first] + second + [third]:
+        copy.wait_send()
+    for copy in outs:
+        copy.wait()
+
+
+def factor_kernel(used_ref, gram_ref, panel_ref, got_ref, left_ref, low_ref, fact_ref, aug):
+    mats, rank = gram_ref.shape[0], gram_ref.shape[1]
+    block = 32
+    row_at = lax.broadcasted_iota(jnp.int32, (rank, rank), 0)
+    col_at = lax.broadcasted_iota(jnp.int32, (rank, rank), 1)
+    eye = (row_at == col_at).astype(jnp.float32)
+    for m in range(mats):
+        aug[m, :, :rank] = gram_ref[m] + ridge_term * eye
+        aug[m, :, rank:] = eye
+    small_row = lax.broadcasted_iota(jnp.int32, (mats, block, block), 1)
+    small_col = lax.broadcasted_iota(jnp.int32, (mats, block, block), 2)
+    small_eye = (small_row == small_col).astype(jnp.float32)
+    for start in range(0, rank, block):
+        stop = start + block
+
+        def eliminate(k, carry):
+            left, right = carry
+            on_row = small_row == k
+            left_row = jnp.sum(jnp.where(on_row, left, 0.0), axis=1, keepdims=True)
+            right_row = jnp.sum(jnp.where(on_row, right, 0.0), axis=1, keepdims=True)
+            column = jnp.sum(jnp.where(small_col == k, left, 0.0), axis=2, keepdims=True)
+            pivot = jnp.sum(jnp.where(small_col[:, :1] == k, left_row, 0.0), axis=2, keepdims=True)
+            ratio = jnp.where(small_row > k, column / pivot, 0.0)
+            return left - ratio * left_row, right - ratio * right_row
+
+        left, right = lax.fori_loop(
+            0, block, eliminate, (aug[:, start:stop, start:stop], small_eye)
+        )
+        diagonal = jnp.sum(left * small_eye, axis=2, keepdims=True)
+        inverse = right * lax.rsqrt(diagonal)
+        for m in range(mats):
+            top = jnp.dot(inverse[m], aug[m, start:stop, :], precision=HIGHEST, preferred_element_type=jnp.float32)
+            aug[m, start:stop, :] = top
+            if stop < rank:
+                below = top[:, :rank].T[stop:]
+                aug[m, stop:, :] -= jnp.dot(below, top, precision=HIGHEST, preferred_element_type=jnp.float32)
+    scale = math.sqrt(D)
+    for m in range(mats):
+        ortho = jnp.dot(
+            panel_ref[m], aug[m, :, rank:].T, precision=HIGHEST, preferred_element_type=jnp.float32
+        )
+        left_ref[m] = jnp.where(used_ref[m] > 0, ortho * scale, 0.0)
+        low = ortho.astype(jnp.bfloat16)
+        low_ref[m] = low
+        fact_ref[m] = jnp.dot(low.T, got_ref[m], preferred_element_type=jnp.float32)
+
+
+def reduce_kernel(
+    shards_f, groups, kinds, experts,
+    slot_ref, part_ref,
+    fact_out, right_out,
+    pairbuf, halfbuf, chipbuf, lowbuf, newbuf, retbuf, pickbuf, rightbuf,
+    a_send, a_recv, b_send, b_recv, c_send, c_recv, d_send, d_recv, e_send, e_recv,
+):
+    mats, rank, hidden = part_ref.shape
+    f, z = greet(shards_f, groups)
+    core = lax.rem(f, 2)
+    chip = f // 2
+    chips = shards_f // 2
+    pair = chip * 2 + 1 - core
+    half = rank // 2
+    piece = rank // shards_f
+    columns = hidden // groups
+
+    first = []
+    for m in range(mats):
+        src = part_ref.at[m, pl.ds(pl.multiple_of((1 - core) * half, half), half), :]
+        copy = remote(src, pairbuf.at[m], a_send.at[m], a_recv.at[m], pair, z)
+        copy.start()
+        first.append(copy)
+    second = []
+    own = pl.ds(pl.multiple_of(core * half, half), half)
+    for m in range(mats):
+        first[m].wait_recv()
+        halfbuf[m] = part_ref[m, own, :] + pairbuf[m]
+        for j in (2, 1, 3):
+            other = lax.rem(chip + j, chips)
+            copy = remote(
+                halfbuf.at[m, pl.ds(pl.multiple_of(other * piece, piece), piece), :],
+                chipbuf.at[j - 1, m],
+                b_send.at[j - 1, m],
+                b_recv.at[j - 1, m],
+                other * 2 + core,
+                z,
+            )
+            copy.start()
+            second.append(copy)
+    chunk = core * half + chip * piece
+    at = pl.ds(pl.multiple_of(chunk, piece), piece)
+    mine = pl.ds(pl.multiple_of(chip * piece, piece), piece)
+    third = []
+    for copy in second:
+        copy.wait_recv()
+    for m in range(mats):
+        total = halfbuf[m, mine, :]
+        for j in range(1, chips):
+            total = total + chipbuf[j - 1, m]
+        lowbuf[m, at, :] = total.astype(jnp.bfloat16)
+        mean_square = jnp.mean(total * total, axis=1, keepdims=True)
+        fresh = total * lax.rsqrt(mean_square + epsilon)
+        for t in range(groups):
+            newbuf[t, m] = fresh[:, t * columns : (t + 1) * columns]
+    fourth = []
+    for j in range(1, groups):
+        d = lax.rem(z + j, groups)
+        copy = remote(newbuf.at[d], retbuf.at[z], d_send.at[j - 1], d_recv.at[j - 1], f, d)
+        copy.start()
+        fourth.append(copy)
+    for j in range(1, shards_f):
+        part = lowbuf.at[:, at, :]
+        copy = remote(part, part, c_send.at[j - 1], c_recv.at[j - 1], lax.rem(f + j, shards_f), z)
+        copy.start()
+        third.append(copy)
+    retbuf[z] = newbuf[z]
+    for j in range(1, groups):
+        source = lax.rem(z + groups - j, groups)
+        remote(newbuf.at[source], retbuf.at[source], d_send.at[j - 1], d_recv.at[j - 1], f, z).wait_recv()
+    for e in range(experts):
+        slot = slot_ref[e]
+        owner = slot // CAP
+        position = lax.rem(slot, CAP)
+        for k in range(kinds):
+            rightbuf[e * kinds + k, at, :] = retbuf[owner, position * kinds + k]
+    fifth = []
+    for j in range(1, shards_f):
+        part = rightbuf.at[:, at, :]
+        copy = remote(part, part, e_send.at[j - 1], e_recv.at[j - 1], lax.rem(f + j, shards_f), z)
+        copy.start()
+        fifth.append(copy)
+    for buffer, send, recv in ((lowbuf, c_send, c_recv), (rightbuf, e_send, e_recv)):
+        for j in range(1, shards_f):
+            source = lax.rem(f + shards_f - j, shards_f)
+            place = lax.rem(source, 2) * half + (source // 2) * piece
+            part = buffer.at[:, pl.ds(pl.multiple_of(place, piece), piece), :]
+            remote(part, part, send.at[j - 1], recv.at[j - 1], f, z).wait_recv()
+    fact_out[...] = lowbuf[...]
+    right_out[...] = rightbuf[...]
+    for copy in first + second + third + fourth + fifth:
+        copy.wait_send()
+
+
+def fresh_kernel(used_ref, got_ref, low_ref, fact_ref, state_ref):
+    m = pl.program_id(0)
+    update = jnp.dot(low_ref[0], fact_ref[0], preferred_element_type=jnp.float32)
+    fresh = got_ref[0].astype(jnp.float32) - feedback * update
+    state_ref[0] = jnp.where(used_ref[m] > 0, fresh, 0.0).astype(jnp.bfloat16)
+
+
+def shards(momentum, gradient, right_in, owners):
+    groups = lax.axis_size("tensor")
+    shards_f = lax.axis_size("fsdp")
+    experts, kinds, rows, columns = momentum.shape
+    rank = right_in.shape[-1]
+    hidden = groups * columns
+    mats = CAP * kinds
+    z = lax.axis_index("tensor")
+    index_line = jnp.arange(experts, dtype=jnp.int32)
+    same_owner = owners[:, None] == owners[None, :]
+    earlier = index_line[None, :] < index_line[:, None]
+    position = jnp.sum((same_owner & earlier).astype(jnp.int32), axis=1)
+    slot = owners * CAP + position
+    hit = slot[:, None] == jnp.arange(groups * CAP, dtype=jnp.int32)[None, :]
+    sel = jnp.sum(jnp.where(hit, index_line[:, None], 0), axis=0).astype(jnp.int32)
+    here = slot[:, None] == (z * CAP + jnp.arange(mats, dtype=jnp.int32) // kinds)[None, :]
+    used = jnp.sum(here.astype(jnp.int32), axis=0)
+
+    smem = pl.BlockSpec(memory_space=pltpu.SMEM)
+    vmem = pl.BlockSpec(memory_space=pltpu.VMEM)
+    hbm = pl.BlockSpec(memory_space=pl.ANY)
+    f32, bf16 = jnp.float32, jnp.bfloat16
+    shape = jax.ShapeDtypeStruct
+    dma = pltpu.SemaphoreType.DMA
+    remote_slots = (groups - 1) * CAP
+    chips = shards_f // 2
+
+    got, panel, gram = pl.pallas_call(
+        functools.partial(exchange_kernel, shards_f, groups, kinds),
+        out_shape=(shape((mats, rows, hidden), bf16), shape((mats, rows, rank), f32), shape((mats, rank, rank), f32)),
+        in_specs=[smem, vmem, vmem, vmem],
+        out_specs=(hbm, vmem, vmem),
+        scratch_shapes=[
+            pltpu.VMEM((remote_slots, kinds, rows, columns), bf16),
+            pltpu.VMEM((mats, rows, hidden), bf16),
+            pltpu.VMEM((groups, experts * kinds, columns, rank), bf16),
+            pltpu.VMEM((mats, rank, rank), f32),
+            pltpu.VMEM((mats // 2, rank, rank), f32),
+            pltpu.VMEM((mats // 2, rank, rank), f32),
+            pltpu.VMEM((chips - 1, mats // 2, rank, rank), f32),
+            pltpu.VMEM((mats, rank, rank), f32),
+            dma((remote_slots,)), dma((remote_slots,)),
+            dma((groups - 1,)), dma((groups - 1,)),
+            dma((shards_f - 1,)), dma((shards_f - 1,)),
+            dma((chips + 1,)), dma((chips + 1,)),
+            dma((groups * CAP,)),
+        ],
+        compiler_params=pltpu.CompilerParams(
+            collective_id=0, has_side_effects=True, vmem_limit_bytes=VMEM_BYTES
+        ),
+        name="exchange",
+    )(sel, momentum, gradient, right_in.reshape(experts * kinds, columns, rank))
+
+    left, low, part = pl.pallas_call(
+        factor_kernel,
+        out_shape=(shape((mats, rows, rank), f32), shape((mats, rows, rank), bf16), shape((mats, rank, hidden), f32)),
+        in_specs=[smem, vmem, vmem, vmem],
+        out_specs=(vmem, vmem, vmem),
+        scratch_shapes=[pltpu.VMEM((mats, rank, 2 * rank), f32)],
+        compiler_params=pltpu.CompilerParams(vmem_limit_bytes=VMEM_BYTES),
+        name="factors",
+    )(used, gram, panel, got)
+
+    piece = rank // shards_f
+    fact, right = pl.pallas_call(
+        functools.partial(reduce_kernel, shards_f, groups, kinds, experts),
+        out_shape=(shape((mats, rank, hidden), bf16), shape((experts * kinds, rank, columns), f32)),
+        in_specs=[smem, vmem],
+        out_specs=(vmem, vmem),
+        scratch_shapes=[
+            pltpu.VMEM((mats, rank // 2, hidden), f32),
+            pltpu.VMEM((mats, rank // 2, hidden), f32),
+            pltpu.VMEM((chips - 1, mats, piece, hidden), f32),
+            pltpu.VMEM((mats, rank, hidden), bf16),
+            pltpu.VMEM((groups, mats, piece, columns), f32),
+            pltpu.VMEM((groups, mats, piece, columns), f32),
+            pltpu.VMEM((8, 128), f32),
+            pltpu.VMEM((experts * kinds, rank, columns), f32),
+            dma((mats,)), dma((mats,)),
+            dma((chips - 1, mats)), dma((chips - 1, mats)),
+            dma((shards_f - 1,)), dma((shards_f - 1,)),
+            dma((groups - 1,)), dma((groups - 1,)),
+            dma((shards_f - 1,)), dma((shards_f - 1,)),
+        ],
+        compiler_params=pltpu.CompilerParams(
+            collective_id=1, has_side_effects=True, vmem_limit_bytes=VMEM_BYTES
+        ),
+        name="reduce",
+    )(slot, part)
+
+    band = min(rows, 256)
+    state = pl.pallas_call(
+        fresh_kernel,
+        grid=(mats, rows // band),
+        out_shape=shape((mats, rows, hidden), bf16),
+        in_specs=[
+            smem,
+            pl.BlockSpec((1, band, hidden), lambda m, i: (m, i, 0)),
+            pl.BlockSpec((1, band, rank), lambda m, i: (m, i, 0)),
+            pl.BlockSpec((1, rank, hidden), lambda m, i: (m, 0, 0)),
+        ],
+        out_specs=pl.BlockSpec((1, band, hidden), lambda m, i: (m, i, 0)),
+        name="fresh",
+    )(used, got, low, fact)
+    right_new = jnp.swapaxes(right, 1, 2).reshape(experts, kinds, columns, rank)
+    return (
+        state.reshape(CAP, kinds, rows, hidden),
+        left.reshape(CAP, kinds, rows, rank),
+        right_new,
+    )
+
+
 def solution(mesh):
+    fits = mesh.shape["fsdp"] == 8 and mesh.shape["tensor"] == 4
     return jax.shard_map(
-        shards,
+        shards if fits else general_shards,
         mesh=mesh,
         in_specs=(
             P(None, None, "fsdp", "tensor"),

time: 531 us -> 269 us (0.51)
  waiting for transfers between devices: 320 us -> 0 us
  Pallas kernels: 0 us -> 262 us
  other arithmetic: 98.1 us -> 2.84 us
  local copies, waits for them, and re-layouts: 44.3 us -> 1.39 us
  matrix products: 37.6 us -> 0 us
  starting transfers between devices: 15.1 us -> 0 us
  between operations: 14.2 us -> 0.68 us
    pallas_call x0 -> x4, Pallas kernels: none -> 262 us  [the longest x1 130 us: shards(): pl.pallas_call(functools.partial(exchange_kernel, shards_f, groups, kinds...]
    all_to_all x3 -> x0, waiting for transfers between devices: 199 us -> none  [the longest x1 136 us: shards(): lax.all_to_all(send_state, 'tensor', split_axis=3, concat_axis=3, tiled=T...]
    psum x2 -> x0, waiting for transfers between devices: 121 us -> none  [the longest x1 69 us: shards(): factor = lax.psum(factor_part, 'fsdp')]
    another operation x7 -> x0, other arithmetic: 86.6 us -> none  [the longest x4 47.1 us: orthonormal(): lower_factor = jnp.linalg.cholesky(gram_total + ridge_term * eye_matrix)]
    dot_general x7 -> x0, matrix products: 36.6 us -> none  [the longest x1 14.4 us: shards(): update = jnp.einsum('cmrq,cmktq->cmrtk', ortho, factor, precision=highest)]
    all_to_all x2 -> x0, local copies, waits for them, and re-layouts: 19.4 us -> none  [the longest x1 16.1 us: shards(): lax.all_to_all(send_state, 'tensor', split_axis=3, concat_axis=3, tiled=T...]
    all_to_all x3 -> x0, starting transfers between devices: 14.9 us -> none  [the longest x1 6.45 us: shards(): lax.all_to_all(send_state, 'tensor', split_axis=3, concat_axis=3, tiled=T...]
    unnamed x9 -> x5, local copies, waits for them, and re-layouts: 13.7 us -> 1.39 us
  transfers between devices with their start and end apart: 5 -> 0, of which waited for: 5 -> 0; matrix products, arithmetic and copies ran while one was open for 9% -> 0% of each run, Pallas kernels for 0% -> 0%
where the time goes in v1:
time: 269 us; the launch traced here: 267 us
  Pallas kernels  262 us (97%)
  other arithmetic  2.84 us (1%)
    pallas_call x1, Pallas kernels, shards(): pl.pallas_call(functools.partial(exchange_kernel, shards_f, groups, kinds...  130 us
    pallas_call x1, Pallas kernels, shards(): pl.pallas_call(functools.partial(reduce_kernel, shards_f, groups, kinds,...  90.2 us
    pallas_call x1, Pallas kernels, shards(): pl.pallas_call(factor_kernel, out_shape=(shape((mats, rows, rank), f32),...  32 us
    pallas_call x1, Pallas kernels, shards(): pl.pallas_call(fresh_kernel, grid=(mats, rows // band), out_shape=shape((...  9.82 us

profile of v1, /device:TPU:0, one launch (start us, length us, event | category | flops | bytes accessed | tf_op | source)
XLA Modules:
  0.0 267.3 jit_solution(16656386787648868431)
XLA Ops:
  0.6 0.9 convert_reduce_fusion.1
  1.6 0.7 multiply_add_fusion.slot_ref
  2.2 0.0 copy-start.1
  2.2 0.7 convert_reduce_fusion.used_ref
  2.9 0.6 select_reduce_fusion.sel_ref
  3.5 130.4 %exchange.1 = (bf16[4,512,1536]{2,1,0:T(8,128)(2,1)}, f32[4,512,128]{2,1,0:T(8,128)}, f32[4,128,128]{2,1,0:T(8,128)}) custom-call(s32[8]{0:T(128)} %select_reduce_fusion.sel_ref, bf16[3,2,512,384]{3,2,1,0:T(8,128)(2,1)} %m_ref.1, bf16[3,2,512,384]{3,2,1,0:T(8,128)(2,1)} %g_ref.1, bf16[6,384,128]{2,1,0:T(8,128)(2,1)} %bitcast.8), custom_call_target="tpu_custom_call" | custom-call | tf_op jit(solution)/shard_map/exchange/pallas_call | solution.py:421
  133.9 0.0 copy-done.1
  133.9 32.0 %factors.1 = (f32[4,512,128]{2,1,0:T(8,128)}, bf16[4,512,128]{2,1,0:T(8,128)(2,1)}, f32[4,128,1536]{2,1,0:T(8,128)}) custom-call(s32[4]{0:T(128)} %convert_reduce_fusion.used_ref, f32[4,128,128]{2,1,0:T(8,128)} %get-tuple-element.12.gram_ref, f32[4,512,128]{2,1,0:T(8,128)} %get-tuple-element.13.panel_ref, bf16[4,512,1536]{2,1,0:T(8,128)(2,1)} %get-tuple-element.11.got_ref), custom_call_target="tpu_custom_call" | custom-call | tf_op jit(solution)/shard_map/factors/pallas_call | solution.py:447
  165.9 90.2 %reduce.1 = (bf16[4,128,1536]{2,1,0:T(8,128)(2,1)}, f32[6,128,384]{2,1,0:T(8,128)}) custom-call(s32[3]{0:T(128)} %copy-done.1, f32[4,128,1536]{2,1,0:T(8,128)} %get-tuple-element.15.part_ref), custom_call_target="tpu_custom_call" | custom-call | tf_op jit(solution)/shard_map/reduce/pallas_call | solution.py:458
  256.1 0.0 copy-start
  256.1 9.8 %fresh.1 = bf16[4,512,1536]{2,1,0:T(8,128)(2,1)} custom-call(s32[4]{0:T(128)} %convert_reduce_fusion.used_ref, bf16[4,512,1536]{2,1,0:T(8,128)(2,1)} %get-tuple-element.11.got_ref, bf16[4,512,128]{2,1,0:T(8,128)(2,1)} %get-tuple-element.14.low_ref, bf16[4,128,1536]{2,1,0:T(8,128)(2,1)} %get-tuple-element.16.fact_ref), custom_call_target="tpu_custom_call" | custom-call | tf_op jit(solution)/shard_map/fresh/pallas_call | solution.py:485
  266.0 0.0 copy-done
  266.0 1.4 copy.8
  (1 shorter events, 0.0 us)
Async XLA Ops:
  2.2 131.7 %copy-start.1 = (s32[3]{0:T(128)}, s32[3]{0:T(128)S(1)}, u32[]{:S(2)}) copy-start(s32[3]{0:T(128)S(1)} %multiply_add_fusion.slot_ref) | copy-start | bytes 40
  256.1 9.8 %copy-start = (f32[6,128,384]{2,1,0:T(8,128)S(1)}, f32[6,128,384]{2,1,0:T(8,128)}, u32[]{:S(2)}) copy-start(f32[6,128,384]{2,1,0:T(8,128)} %get-tuple-element.18) | copy-start | bytes 3538948

commit v2 on v0

--- a/solution.py
+++ b/solution.py
@@ -1,8 +1,11 @@
+import functools
 import math
 
 import jax
 import jax.numpy as jnp
 from jax import lax
+from jax.experimental import pallas as pl
+from jax.experimental.pallas import tpu as pltpu
 from jax.sharding import PartitionSpec as P
 
 D = 4096
@@ -34,7 +37,7 @@
     return (owner_hit & slot_hit).astype(jnp.float32)
 
 
-def shards(momentum, gradient, right_in, owners):
+def general_shards(momentum, gradient, right_in, owners):
     highest = lax.Precision.HIGHEST
     groups = lax.axis_size("tensor")
     rows = momentum.shape[2]
@@ -75,9 +78,466 @@
     return (state_out, left_out, right_out)
 
 
+MESH = pl.DeviceIdType.MESH
+HIGHEST = lax.Precision.HIGHEST
+VMEM_BYTES = 56 * 1024 * 1024
+
+
+def greet(shards_f, groups):
+    f = lax.axis_index("fsdp")
+    z = lax.axis_index("tensor")
+    barrier = pltpu.get_barrier_semaphore()
+    for j in range(1, shards_f):
+        pl.semaphore_signal(
+            barrier, inc=1, device_id={"fsdp": lax.rem(f + j, shards_f), "tensor": z}, device_id_type=MESH
+        )
+    for j in range(1, groups):
+        pl.semaphore_signal(
+            barrier, inc=1, device_id={"fsdp": f, "tensor": lax.rem(z + j, groups)}, device_id_type=MESH
+        )
+    pl.semaphore_wait(barrier, shards_f - 1 + groups - 1)
+    return f, z
+
+
+def remote(src, dst, send_sem, recv_sem, f, z):
+    return pltpu.make_async_remote_copy(
+        src_ref=src,
+        dst_ref=dst,
+        send_sem=send_sem,
+        recv_sem=recv_sem,
+        device_id={"fsdp": f, "tensor": z},
+        device_id_type=MESH,
+    )
+
+
+def inverse_factor(aug, mats, rank):
+    block = 32
+    small_row = lax.broadcasted_iota(jnp.int32, (mats, block, block), 1)
+    small_col = lax.broadcasted_iota(jnp.int32, (mats, block, block), 2)
+    small_eye = (small_row == small_col).astype(jnp.float32)
+    for start in range(0, rank, block):
+        stop = start + block
+
+        def eliminate(k, carry):
+            left, right = carry
+            on_row = small_row == k
+            left_row = jnp.sum(jnp.where(on_row, left, 0.0), axis=1, keepdims=True)
+            right_row = jnp.sum(jnp.where(on_row, right, 0.0), axis=1, keepdims=True)
+            column = jnp.sum(jnp.where(small_col == k, left, 0.0), axis=2, keepdims=True)
+            pivot = jnp.sum(jnp.where(small_col[:, :1] == k, left_row, 0.0), axis=2, keepdims=True)
+            ratio = jnp.where(small_row > k, column / pivot, 0.0)
+            return left - ratio * left_row, right - ratio * right_row
+
+        left, right = lax.fori_loop(
+            0, block, eliminate, (aug[:, start:stop, start:stop], small_eye)
+        )
+        diagonal = jnp.sum(left * small_eye, axis=2, keepdims=True)
+        inverse = right * lax.rsqrt(diagonal)
+        for m in range(mats):
+            top = jnp.dot(inverse[m], aug[m, start:stop, :], precision=HIGHEST, preferred_element_type=jnp.float32)
+            aug[m, start:stop, :] = top
+            if stop < rank:
+                below = top[:, :rank].T[stop:]
+                aug[m, stop:, :] -= jnp.dot(below, top, precision=HIGHEST, preferred_element_type=jnp.float32)
+
+
+def step_kernel(
+    shards_f, groups,
+    sel_ref, m_ref, g_ref, r_ref,
+    got_out, low_out, fact_out, right_out,
+    summed, sendbuf, got, pbuf, precv, pchunk,
+    gram, gpair, ghalf, gchip, gpiece, gdepth, gfull, aug, wfull,
+    obuf, fpart, fpair, fhalf, fchip, fchunk, fsend, lowbuf, sqbuf, sqrecv, rightbuf,
+    p_send, p_recv, ga_send, ga_recv, gb_send, gb_recv, gc_send, gc_recv, gd_send, gd_recv,
+    w_send, w_recv, o_send, o_recv, fa_send, fa_recv, fb_send, fb_recv, fz_send, fz_recv,
+    sq_send, sq_recv, low_send, low_recv, right_send, right_recv,
+    s_send, first_recv, near_recv, second_recv, pass_send, pass_recv, out_sem,
+):
+    experts, kinds, rows, columns = m_ref.shape
+    mats = experts * kinds
+    slots = CAP * kinds
+    rank = r_ref.shape[-1]
+    half_m = mats // 2
+    f, z = greet(shards_f, groups)
+    core = lax.rem(f, 2)
+    chip = f // 2
+    chips = shards_f // 2
+    pair = chip * 2 + 1 - core
+    zrows = rows // groups
+    started = []
+
+    def go(src, dst, send_sem, recv_sem, to_f, to_z):
+        copy = remote(src, dst, send_sem, recv_sem, to_f, to_z)
+        copy.start()
+        started.append(copy)
+        return copy
+
+    def landed(dst, recv_sem):
+        remote(dst, dst, recv_sem, recv_sem, f, z).wait_recv()
+
+    step = 128
+    zmine = pl.ds(pl.multiple_of(z * zrows, zrows), zrows)
+    for e in range(experts):
+        for k in range(kinds):
+            @pl.loop(0, rows // step)
+            def _(i):
+                at = pl.ds(pl.multiple_of(i * step, step), step)
+                total = m_ref[e, k, at, :].astype(jnp.float32) + g_ref[e, k, at, :].astype(jnp.float32)
+                low = total.astype(jnp.bfloat16)
+                summed[e, k, at, :] = low
+                pbuf[e * kinds + k, at, :] = jnp.dot(low, r_ref[e * kinds + k], preferred_element_type=jnp.float32)
+        for j in (2, 3, 1):
+            d = lax.rem(z + j, groups)
+            go(
+                pbuf.at[pl.ds(e * kinds, kinds), pl.ds(pl.multiple_of(d * zrows, zrows), zrows), :],
+                precv.at[j - 1, pl.ds(e * kinds, kinds)],
+                p_send.at[j - 1, e],
+                p_recv.at[j - 1, e],
+                f,
+                d,
+            )
+
+    near = z + 1 - 2 * lax.rem(z, 2)
+    upper = z // 2
+    inner = 2 - upper
+    outer = 3 - 3 * upper
+    picks = (
+        sel_ref[groups * CAP + 1 - upper],
+        sel_ref[outer * CAP],
+        sel_ref[inner * CAP],
+        sel_ref[near * CAP],
+        sel_ref[near * CAP + 1],
+    )
+    for unit, expert in enumerate(picks):
+        for k in range(kinds):
+            @pl.loop(0, rows // step)
+            def _(i):
+                at = pl.ds(pl.multiple_of(i * step, step), step)
+                sendbuf[unit, k, at, :] = summed[expert, k, at, :]
+    here = pl.ds(pl.multiple_of(z * columns, columns), columns)
+    for c in range(CAP):
+        expert = sel_ref[z * CAP + c]
+        for k in range(kinds):
+            @pl.loop(0, rows // step)
+            def _(i):
+                at = pl.ds(pl.multiple_of(i * step, step), step)
+                got[c * kinds + k, at, here] = summed[expert, k, at, :]
+
+    def place(c, source):
+        return got.at[pl.ds(c * kinds, kinds), :, pl.ds(pl.multiple_of(source * columns, columns), columns)]
+
+    for j in range(1, groups):
+        for e in range(experts):
+            landed(precv.at[j - 1, pl.ds(e * kinds, kinds)], p_recv.at[j - 1, e])
+    go(sendbuf.at[0], place(1, z), s_send.at[0], second_recv.at[lax.rem(z, 2)], f, inner)
+    go(sendbuf.at[4], place(1, z), s_send.at[4], near_recv, f, near)
+
+    for m in range(mats):
+        total = pbuf[m, zmine, :]
+        for j in range(1, groups):
+            total = total + precv[j - 1, m]
+        pchunk[m] = total
+        gram[m] = jnp.dot(total.T, total, precision=HIGHEST, preferred_element_type=jnp.float32)
+    go(gram.at[pl.ds((1 - core) * half_m, half_m)], gpair, ga_send, ga_recv, pair, z).wait_recv()
+    ghalf[...] = gram[pl.ds(core * half_m, half_m)] + gpair[...]
+    prows = rank // chips
+    cmine = pl.ds(pl.multiple_of(chip * prows, prows), prows)
+    for j in (2, 1, 3):
+        other = lax.rem(chip + j, chips)
+        go(
+            ghalf.at[:, pl.ds(pl.multiple_of(other * prows, prows), prows), :],
+            gchip.at[j - 1], gb_send.at[j - 1], gb_recv.at[j - 1], other * 2 + core, z,
+        )
+    total = ghalf[:, cmine, :]
+    for j in range(1, chips):
+        landed(gchip.at[j - 1], gb_recv.at[j - 1])
+        total = total + gchip[j - 1]
+    gpiece[...] = total
+    for j in (2, 3, 1):
+        go(gpiece, gdepth.at[j - 1], gc_send.at[j - 1], gc_recv.at[j - 1], f, lax.rem(z + j, groups))
+    for j in range(1, groups):
+        landed(gdepth.at[j - 1], gc_recv.at[j - 1])
+        total = total + gdepth[j - 1]
+    gfull[:, cmine, :] = total
+    for j in (2, 1, 3):
+        part = gfull.at[:, cmine, :]
+        go(part, part, gd_send.at[j - 1], gd_recv.at[j - 1], lax.rem(chip + j, chips) * 2 + core, z)
+    go(sendbuf.at[1], place(0, z), s_send.at[1], first_recv.at[z], f, outer)
+    go(sendbuf.at[3], place(0, z), s_send.at[3], first_recv.at[z], f, near)
+    for j in range(1, chips):
+        other = lax.rem(chip + chips - j, chips)
+        landed(gfull.at[:, pl.ds(pl.multiple_of(other * prows, prows), prows), :], gd_recv.at[j - 1])
+
+    row_at = lax.broadcasted_iota(jnp.int32, (rank, rank), 0)
+    col_at = lax.broadcasted_iota(jnp.int32, (rank, rank), 1)
+    eye = (row_at == col_at).astype(jnp.float32)
+    for m in range(half_m):
+        aug[m, :, :rank] = gfull[m] + ridge_term * eye
+        aug[m, :, rank:] = eye
+    inverse_factor(aug, half_m, rank)
+    wmine = pl.ds(core * half_m, half_m)
+    wfull[wmine] = aug[:, :, rank:]
+    go(wfull.at[wmine], wfull.at[wmine], w_send, w_recv, pair, z)
+    landed(wfull.at[pl.ds((1 - core) * half_m, half_m)], w_recv)
+
+    for m in range(mats):
+        ortho = jnp.dot(pchunk[m], wfull[m].T, precision=HIGHEST, preferred_element_type=jnp.float32)
+        obuf[m, zmine, :] = ortho.astype(jnp.bfloat16)
+    for j in (2, 3, 1):
+        part = obuf.at[:, zmine, :]
+        go(part, part, o_send.at[j - 1], o_recv.at[j - 1], f, lax.rem(z + j, groups))
+    for j in range(1, groups):
+        source = lax.rem(z + groups - j, groups)
+        landed(obuf.at[:, pl.ds(pl.multiple_of(source * zrows, zrows), zrows), :], o_recv.at[j - 1])
+
+    far = 2 - 2 * upper
+    is_inner = (z == 1) | (z == 2)
+
+    @pl.when(is_inner)
+    def _():
+        for i in range(2):
+            block = place(1, far + i)
+            landed(block, second_recv.at[i])
+            remote(block, block, pass_send.at[i], pass_recv.at[i], f, near).start()
+
+    go(sendbuf.at[2], place(0, z), s_send.at[2], first_recv.at[z], f, inner)
+
+    for m in range(mats):
+        fpart[m] = jnp.dot(obuf[m].T, summed[m // kinds, m % kinds], preferred_element_type=jnp.float32)
+        low_rows = rank // 2
+        go(
+            fpart.at[m, pl.ds(pl.multiple_of((1 - core) * low_rows, low_rows), low_rows), :],
+            fpair.at[m], fa_send.at[m], fa_recv.at[m], pair, z,
+        )
+    piece = rank // shards_f
+    own = pl.ds(pl.multiple_of(core * low_rows, low_rows), low_rows)
+    for m in range(mats):
+        landed(fpair.at[m], fa_recv.at[m])
+        fhalf[m] = fpart[m, own, :] + fpair[m]
+    for j in (2, 1, 3):
+        other = lax.rem(chip + j, chips)
+        go(
+            fhalf.at[:, pl.ds(pl.multiple_of(other * piece, piece), piece), :],
+            fchip.at[j - 1], fb_send.at[j - 1], fb_recv.at[j - 1], other * 2 + core, z,
+        )
+    total = fhalf[:, pl.ds(pl.multiple_of(chip * piece, piece), piece), :]
+    for j in range(1, chips):
+        landed(fchip.at[j - 1], fb_recv.at[j - 1])
+        total = total + fchip[j - 1]
+    square = total * total
+    part_sum = square[:, :, :128]
+    for lane in range(128, columns, 128):
+        part_sum = part_sum + square[:, :, lane : lane + 128]
+    sqbuf[...] = part_sum
+    for j in (2, 3, 1):
+        go(sqbuf, sqrecv.at[j - 1], sq_send.at[j - 1], sq_recv.at[j - 1], f, lax.rem(z + j, groups))
+    fchunk[...] = total
+    chunk = core * low_rows + chip * piece
+    at = pl.ds(pl.multiple_of(chunk, piece), piece)
+    for j in (2, 3, 1):
+        d = lax.rem(z + j, groups)
+        for c in range(CAP):
+            expert = sel_ref[d * CAP + c]
+            for k in range(kinds):
+                fsend[j - 1, c * kinds + k] = fchunk[expert * kinds + k].astype(jnp.bfloat16)
+        go(fsend.at[j - 1], lowbuf.at[:, at, here], fz_send.at[j - 1], fz_recv.at[j - 1], f, d)
+    for c in range(CAP):
+        expert = sel_ref[z * CAP + c]
+        for k in range(kinds):
+            lowbuf[c * kinds + k, at, here] = fchunk[expert * kinds + k].astype(jnp.bfloat16)
+    for j in range(1, groups):
+        source = lax.rem(z + groups - j, groups)
+        there = pl.ds(pl.multiple_of(source * columns, columns), columns)
+        landed(lowbuf.at[:, at, there], fz_recv.at[j - 1])
+    for j in range(1, shards_f):
+        part = lowbuf.at[:, at, :]
+        go(part, part, low_send.at[j - 1], low_recv.at[j - 1], lax.rem(f + j, shards_f), z)
+    square = sqbuf[...]
+    for j in range(1, groups):
+        landed(sqrecv.at[j - 1], sq_recv.at[j - 1])
+        square = square + sqrecv[j - 1]
+    mean_square = jnp.sum(square, axis=2, keepdims=True) / (groups * columns)
+    rightbuf[:, at, :] = fchunk[...] * lax.rsqrt(mean_square + epsilon)
+    for j in range(1, shards_f):
+        part = rightbuf.at[:, at, :]
+        go(part, part, right_send.at[j - 1], right_recv.at[j - 1], lax.rem(f + j, shards_f), z)
+    for c in range(CAP):
+        expert = sel_ref[z * CAP + c]
+        for k in range(kinds):
+            low_out[c * kinds + k] = obuf[expert * kinds + k]
+
+    def keep(c, source, sem):
+        block = place(c, source)
+        there = pl.ds(pl.multiple_of(source * columns, columns), columns)
+        pltpu.make_async_copy(block, got_out.at[pl.ds(c * kinds, kinds), :, there], out_sem.at[sem]).start()
+
+    keep(0, z, 0)
+    keep(1, z, 1)
+    landed(place(1, near), near_recv)
+    keep(1, near, 2)
+    for n, source in enumerate((near, far, far + 1)):
+        landed(place(0, source), first_recv.at[source])
+        keep(0, source, 3 + n)
+
+    @pl.when(is_inner)
+    def _():
+        for i in range(2):
+            block = place(1, far + i)
+            remote(block, block, pass_send.at[i], pass_recv.at[i], f, near).wait_send()
+
+    @pl.when(jnp.logical_not(is_inner))
+    def _():
+        for i in range(2):
+            landed(place(1, far + i), pass_recv.at[i])
+
+    for i in range(2):
+        keep(1, far + i, 6 + i)
+    for buffer, recv in ((lowbuf, low_recv), (rightbuf, right_recv)):
+        for j in range(1, shards_f):
+            source = lax.rem(f + shards_f - j, shards_f)
+            start = lax.rem(source, 2) * low_rows + (source // 2) * piece
+            landed(buffer.at[:, pl.ds(pl.multiple_of(start, piece), piece), :], recv.at[j - 1])
+    fact_out[...] = lowbuf[...]
+    right_out[...] = rightbuf[...]
+    for copy in started:
+        copy.wait_send()
+    for n, (c, source) in enumerate(
+        ((0, z), (1, z), (1, near), (0, near), (0, far), (0, far + 1), (1, far), (1, far + 1))
+    ):
+        there = pl.ds(pl.multiple_of(source * columns, columns), columns)
+        pltpu.make_async_copy(
+            place(c, source), got_out.at[pl.ds(c * kinds, kinds), :, there], out_sem.at[n]
+        ).wait()
+
+
+def fresh_kernel(used_ref, got_ref, low_ref, fact_ref, state_ref, left_ref):
+    m = pl.program_id(0)
+    update = jnp.dot(low_ref[0], fact_ref[0], preferred_element_type=jnp.float32)
+    fresh = got_ref[0].astype(jnp.float32) - feedback * update
+    state_ref[0] = jnp.where(used_ref[m] > 0, fresh, 0.0).astype(jnp.bfloat16)
+    left = low_ref[0].astype(jnp.float32) * math.sqrt(D)
+    left_ref[0] = jnp.where(used_ref[m] > 0, left, 0.0)
+
+
+def shards(momentum, gradient, right_in, owners):
+    groups = lax.axis_size("tensor")
+    shards_f = lax.axis_size("fsdp")
+    experts, kinds, rows, columns = momentum.shape
+    rank = right_in.shape[-1]
+    hidden = groups * columns
+    mats = CAP * kinds
+    z = lax.axis_index("tensor")
+    index_line = jnp.arange(experts, dtype=jnp.int32)
+    same_owner = owners[:, None] == owners[None, :]
+    earlier = index_line[None, :] < index_line[:, None]
+    position = jnp.sum((same_owner & earlier).astype(jnp.int32), axis=1)
+    slot = owners * CAP + position
+    hit = slot[:, None] == jnp.arange(groups * CAP, dtype=jnp.int32)[None, :]
+    sel = jnp.sum(jnp.where(hit, index_line[:, None], 0), axis=0).astype(jnp.int32)
+    second = sel.reshape(groups, CAP)[:, 1] * jnp.sum(hit, axis=0).reshape(groups, CAP)[:, 1]
+    sel = jnp.concatenate([sel, second.reshape(2, groups // 2).sum(axis=1).astype(jnp.int32)])
+    here = slot[:, None] == (z * CAP + jnp.arange(mats, dtype=jnp.int32) // kinds)[None, :]
+    used = jnp.sum(here.astype(jnp.int32), axis=0)
+
+    smem = pl.BlockSpec(memory_space=pltpu.SMEM)
+    vmem = pl.BlockSpec(memory_space=pltpu.VMEM)
+    hbm = pl.BlockSpec(memory_space=pl.ANY)
+    f32, bf16 = jnp.float32, jnp.bfloat16
+    shape = jax.ShapeDtypeStruct
+    dma = pltpu.SemaphoreType.DMA
+    chips = shards_f // 2
+    every = experts * kinds
+    half_m = every // 2
+    zrows = rows // groups
+    piece = rank // shards_f
+    near_z, near_c, near_f = groups - 1, chips - 1, shards_f - 1
+    got, low, fact, right = pl.pallas_call(
+        functools.partial(step_kernel, shards_f, groups),
+        out_shape=(
+            shape((mats, rows, hidden), bf16),
+            shape((mats, rows, rank), bf16),
+            shape((mats, rank, hidden), bf16),
+            shape((every, rank, columns), f32),
+        ),
+        in_specs=[smem, vmem, vmem, vmem],
+        out_specs=(hbm, vmem, vmem, vmem),
+        scratch_shapes=[
+            pltpu.VMEM((experts, kinds, rows, columns), bf16),
+            pltpu.VMEM((5, kinds, rows, columns), bf16),
+            pltpu.VMEM((mats, rows, hidden), bf16),
+            pltpu.VMEM((every, rows, rank), f32),
+            pltpu.VMEM((near_z, every, zrows, rank), f32),
+            pltpu.VMEM((every, zrows, rank), f32),
+            pltpu.VMEM((every, rank, rank), f32),
+            pltpu.VMEM((half_m, rank, rank), f32),
+            pltpu.VMEM((half_m, rank, rank), f32),
+            pltpu.VMEM((near_c, half_m, rank // chips, rank), f32),
+            pltpu.VMEM((half_m, rank // chips, rank), f32),
+            pltpu.VMEM((near_z, half_m, rank // chips, rank), f32),
+            pltpu.VMEM((half_m, rank, rank), f32),
+            pltpu.VMEM((half_m, rank, 2 * rank), f32),
+            pltpu.VMEM((every, rank, rank), f32),
+            pltpu.VMEM((every, rows, rank), bf16),
+            pltpu.VMEM((every, rank, columns), f32),
+            pltpu.VMEM((every, rank // 2, columns), f32),
+            pltpu.VMEM((every, rank // 2, columns), f32),
+            pltpu.VMEM((near_c, every, piece, columns), f32),
+            pltpu.VMEM((every, piece, columns), f32),
+            pltpu.VMEM((near_z, mats, piece, columns), bf16),
+            pltpu.VMEM((mats, rank, hidden), bf16),
+            pltpu.VMEM((every, piece, 128), f32),
+            pltpu.VMEM((near_z, every, piece, 128), f32),
+            pltpu.VMEM((every, rank, columns), f32),
+            dma((near_z, experts)), dma((near_z, experts)),
+            dma, dma,
+            dma((near_c,)), dma((near_c,)),
+            dma((near_z,)), dma((near_z,)),
+            dma((near_c,)), dma((near_c,)),
+            dma, dma,
+            dma((near_z,)), dma((near_z,)),
+            dma((every,)), dma((every,)),
+            dma((near_c,)), dma((near_c,)),
+            dma((near_z,)), dma((near_z,)),
+            dma((near_z,)), dma((near_z,)),
+            dma((near_f,)), dma((near_f,)),
+            dma((near_f,)), dma((near_f,)),
+            dma((5,)), dma((groups,)), dma, dma((2,)), dma((2,)), dma((2,)), dma((8,)),
+        ],
+        compiler_params=pltpu.CompilerParams(
+            collective_id=0, has_side_effects=True, vmem_limit_bytes=VMEM_BYTES
+        ),
+        name="step",
+    )(sel, momentum, gradient, right_in.reshape(every, columns, rank))
+
+    band = min(rows, 256)
+    state, left = pl.pallas_call(
+        fresh_kernel,
+        grid=(mats, rows // band),
+        out_shape=(shape((mats, rows, hidden), bf16), shape((mats, rows, rank), f32)),
+        in_specs=[
+            smem,
+            pl.BlockSpec((1, band, hidden), lambda m, i: (m, i, 0)),
+            pl.BlockSpec((1, band, rank), lambda m, i: (m, i, 0)),
+            pl.BlockSpec((1, rank, hidden), lambda m, i: (m, 0, 0)),
+        ],
+        out_specs=(
+            pl.BlockSpec((1, band, hidden), lambda m, i: (m, i, 0)),
+            pl.BlockSpec((1, band, rank), lambda m, i: (m, i, 0)),
+        ),
+        name="fresh",
+    )(used, got, low, fact)
+    right_new = jnp.swapaxes(right, 1, 2).reshape(experts, kinds, columns, rank)
+    return (
+        state.reshape(CAP, kinds, rows, hidden),
+        left.reshape(CAP, kinds, rows, rank),
+        right_new,
+    )
+
+
 def solution(mesh):
+    fits = mesh.shape["fsdp"] == 8 and mesh.shape["tensor"] == 4
     return jax.shard_map(
-        shards,
+        shards if fits else general_shards,
         mesh=mesh,
         in_specs=(
             P(None, None, "fsdp", "tensor"),

time: 531 us -> 237 us (0.45)
  waiting for transfers between devices: 320 us -> 0 us
  Pallas kernels: 0 us -> 230 us
  other arithmetic: 98.1 us -> 3.16 us
  local copies, waits for them, and re-layouts: 44.3 us -> 1.64 us
  matrix products: 37.6 us -> 0 us
  starting transfers between devices: 15.1 us -> 0 us
  between operations: 14.2 us -> 0.66 us
    pallas_call x0 -> x2, Pallas kernels: none -> 230 us  [the longest x1 220 us: shards(): pl.pallas_call(functools.partial(step_kernel, shards_f, groups), out_shap...]
    all_to_all x3 -> x0, waiting for transfers between devices: 199 us -> none  [the longest x1 136 us: shards(): lax.all_to_all(send_state, 'tensor', split_axis=3, concat_axis=3, tiled=T...]
    psum x2 -> x0, waiting for transfers between devices: 121 us -> none  [the longest x1 69 us: shards(): factor = lax.psum(factor_part, 'fsdp')]
    another operation x7 -> x0, other arithmetic: 86.6 us -> none  [the longest x4 47.1 us: orthonormal(): lower_factor = jnp.linalg.cholesky(gram_total + ridge_term * eye_matrix)]
    dot_general x7 -> x0, matrix products: 36.6 us -> none  [the longest x1 14.4 us: shards(): update = jnp.einsum('cmrq,cmktq->cmrtk', ortho, factor, precision=highest)]
    all_to_all x2 -> x0, local copies, waits for them, and re-layouts: 19.4 us -> none  [the longest x1 16.1 us: shards(): lax.all_to_all(send_state, 'tensor', split_axis=3, concat_axis=3, tiled=T...]
    all_to_all x3 -> x0, starting transfers between devices: 14.9 us -> none  [the longest x1 6.45 us: shards(): lax.all_to_all(send_state, 'tensor', split_axis=3, concat_axis=3, tiled=T...]
    unnamed x9 -> x3, local copies, waits for them, and re-layouts: 13.7 us -> 1.39 us
  transfers between devices with their start and end apart: 5 -> 0, of which waited for: 5 -> 0; matrix products, arithmetic and copies ran while one was open for 9% -> 0% of each run, Pallas kernels for 0% -> 0%
where the time goes in v2:
time: 237 us; the launch traced here: 235 us
  Pallas kernels  230 us (97%)
  other arithmetic  3.16 us (1%)
    pallas_call x1, Pallas kernels, shards(): pl.pallas_call(functools.partial(step_kernel, shards_f, groups), out_shap...  220 us
    pallas_call x1, Pallas kernels, shards(): pl.pallas_call(fresh_kernel, grid=(mats, rows // band), out_shape=(shape(...  10.2 us

profile of v2, /device:TPU:0, one launch (start us, length us, event | category | flops | bytes accessed | tf_op | source)
XLA Modules:
  0.0 235.4 jit_solution(2220775001228231256)
XLA Ops:
  0.6 0.9 convert_reduce_fusion.2
  1.6 0.7 multiply_add_fusion
  2.2 0.6 convert_reduce_fusion.1.used_ref
  2.8 0.1 select_reduce_fusion
  2.9 0.1 reshape.46
  3.0 0.1 reshape.45
  3.1 0.2 multiply_reduce_fusion
  3.3 0.1 mul.20
  3.3 0.1 reduce_sum.49
  3.5 0.6 pad_add_fusion.sel_ref
  4.1 219.8 %step.1 = (bf16[4,512,1536]{2,1,0:T(8,128)(2,1)}, bf16[4,512,128]{2,1,0:T(8,128)(2,1)}, bf16[4,128,1536]{2,1,0:T(8,128)(2,1)}, f32[6,128,384]{2,1,0:T(8,128)}) custom-call(s32[10]{0:T(128)} %pad_add_fusion.sel_ref, bf16[3,2,512,384]{3,2,1,0:T(8,128)(2,1)} %m_ref.1, bf16[3,2,512,384]{3,2,1,0:T(8,128)(2,1)} %g_ref.1, bf16[6,384,128]{2,1,0:T(8,128)(2,1)} %bitcast.7), custom_call_target="tpu_custom_call" | custom-call | tf_op jit(solution)/shard_map/step/pallas_call | solution.py:454
  223.8 0.0 copy-start
  223.8 10.2 %fresh.1 = (bf16[4,512,1536]{2,1,0:T(8,128)(2,1)}, f32[4,512,128]{2,1,0:T(8,128)}) custom-call(s32[4]{0:T(128)} %convert_reduce_fusion.1.used_ref, bf16[4,512,1536]{2,1,0:T(8,128)(2,1)} %get-tuple-element.9.got_ref, bf16[4,512,128]{2,1,0:T(8,128)(2,1)} %get-tuple-element.10.low_ref, bf16[4,128,1536]{2,1,0:T(8,128)(2,1)} %get-tuple-element.11.fact_ref), custom_call_target="tpu_custom_call" | custom-call | tf_op jit(solution)/shard_map/fresh/pallas_call | solution.py:513
  234.0 0.0 copy-done
  234.0 1.4 copy.9
  (1 shorter events, 0.0 us)
Async XLA Ops:
  223.8 10.2 %copy-start = (f32[6,128,384]{2,1,0:T(8,128)S(1)}, f32[6,128,384]{2,1,0:T(8,128)}, u32[]{:S(2)}) copy-start(f32[6,128,384]{2,1,0:T(8,128)} %get-tuple-element.14) | copy-start | bytes 3538948

commit v3 on v2

--- a/solution.py
+++ b/solution.py
@@ -112,27 +112,26 @@
 
 def inverse_factor(aug, mats, rank):
     block = 32
-    small_row = lax.broadcasted_iota(jnp.int32, (mats, block, block), 1)
-    small_col = lax.broadcasted_iota(jnp.int32, (mats, block, block), 2)
-    small_eye = (small_row == small_col).astype(jnp.float32)
+    wide = (mats, block, 2 * block)
+    wide_row = lax.broadcasted_iota(jnp.int32, wide, 1)
+    wide_col = lax.broadcasted_iota(jnp.int32, wide, 2)
+    on_diagonal = wide_row == wide_col
+    small = (mats, block, block)
+    small_eye = (lax.broadcasted_iota(jnp.int32, small, 1) == lax.broadcasted_iota(jnp.int32, small, 2)).astype(jnp.float32)
     for start in range(0, rank, block):
         stop = start + block
 
-        def eliminate(k, carry):
-            left, right = carry
-            on_row = small_row == k
-            left_row = jnp.sum(jnp.where(on_row, left, 0.0), axis=1, keepdims=True)
-            right_row = jnp.sum(jnp.where(on_row, right, 0.0), axis=1, keepdims=True)
-            column = jnp.sum(jnp.where(small_col == k, left, 0.0), axis=2, keepdims=True)
-            pivot = jnp.sum(jnp.where(small_col[:, :1] == k, left_row, 0.0), axis=2, keepdims=True)
-            ratio = jnp.where(small_row > k, column / pivot, 0.0)
-            return left - ratio * left_row, right - ratio * right_row
-
-        left, right = lax.fori_loop(
-            0, block, eliminate, (aug[:, start:stop, start:stop], small_eye)
-        )
-        diagonal = jnp.sum(left * small_eye, axis=2, keepdims=True)
-        inverse = right * lax.rsqrt(diagonal)
+        def eliminate(k, both):
+            row = jnp.sum(jnp.where(wide_row == k, both, 0.0), axis=1, keepdims=True)
+            column = jnp.sum(jnp.where(wide_col == k, both, 0.0), axis=2, keepdims=True)
+            pivot = jnp.sum(jnp.where(wide_col[:, :1] == k, row, 0.0), axis=2, keepdims=True)
+            ratio = jnp.where(wide_row[:, :, :1] > k, column * (1.0 / pivot), 0.0)
+            return both - ratio * row
+
+        both = jnp.concatenate([aug[:, start:stop, start:stop], small_eye], axis=2)
+        both = lax.fori_loop(0, block, eliminate, both, unroll=4)
+        diagonal = jnp.sum(jnp.where(on_diagonal, both, 0.0), axis=2, keepdims=True)
+        inverse = both[:, :, block:] * lax.rsqrt(diagonal)
         for m in range(mats):
             top = jnp.dot(inverse[m], aug[m, start:stop, :], precision=HIGHEST, preferred_element_type=jnp.float32)
             aug[m, start:stop, :] = top
@@ -223,14 +222,43 @@
                 at = pl.ds(pl.multiple_of(i * step, step), step)
                 got[c * kinds + k, at, here] = summed[expert, k, at, :]
 
-    def place(c, source):
-        return got.at[pl.ds(c * kinds, kinds), :, pl.ds(pl.multiple_of(source * columns, columns), columns)]
+    def place(c, source, k):
+        return got.at[c * kinds + k, :, pl.ds(pl.multiple_of(source * columns, columns), columns)]
+
+    def send(unit, c, recv, d, k):
+        go(sendbuf.at[unit, k], place(c, z, k), s_send.at[unit, k], recv, f, d)
+
+    def far_second(k):
+        send(0, 1, second_recv.at[lax.rem(z, 2), k], inner, k)
+
+    def far_outer(k):
+        send(1, 0, first_recv.at[z, k], outer, k)
+
+    def far_inner(k):
+        send(2, 0, first_recv.at[z, k], inner, k)
+
+    def near_first(k):
+        send(3, 0, first_recv.at[z, k], near, k)
+
+    def near_second(k):
+        send(4, 1, near_recv.at[k], near, k)
+
+    far = 2 - 2 * upper
+    is_inner = (z == 1) | (z == 2)
+
+    def hand_on(k):
+        @pl.when(is_inner)
+        def _():
+            for i in range(2):
+                block = place(1, far + i, k)
+                landed(block, second_recv.at[i, k])
+                remote(block, block, pass_send.at[i, k], pass_recv.at[i, k], f, near).start()
 
     for j in range(1, groups):
         for e in range(experts):
             landed(precv.at[j - 1, pl.ds(e * kinds, kinds)], p_recv.at[j - 1, e])
-    go(sendbuf.at[0], place(1, z), s_send.at[0], second_recv.at[lax.rem(z, 2)], f, inner)
-    go(sendbuf.at[4], place(1, z), s_send.at[4], near_recv, f, near)
+    far_second(0)
+    near_second(0)
 
     for m in range(mats):
         total = pbuf[m, zmine, :]
@@ -262,11 +290,14 @@
     for j in (2, 1, 3):
         part = gfull.at[:, cmine, :]
         go(part, part, gd_send.at[j - 1], gd_recv.at[j - 1], lax.rem(chip + j, chips) * 2 + core, z)
-    go(sendbuf.at[1], place(0, z), s_send.at[1], first_recv.at[z], f, outer)
-    go(sendbuf.at[3], place(0, z), s_send.at[3], first_recv.at[z], f, near)
     for j in range(1, chips):
         other = lax.rem(chip + chips - j, chips)
         landed(gfull.at[:, pl.ds(pl.multiple_of(other * prows, prows), prows), :], gd_recv.at[j - 1])
+
+    far_second(1)
+    far_outer(0)
+    near_second(1)
+    near_first(0)
 
     row_at = lax.broadcasted_iota(jnp.int32, (rank, rank), 0)
     col_at = lax.broadcasted_iota(jnp.int32, (rank, rank), 1)
@@ -290,17 +321,8 @@
         source = lax.rem(z + groups - j, groups)
         landed(obuf.at[:, pl.ds(pl.multiple_of(source * zrows, zrows), zrows), :], o_recv.at[j - 1])
 
-    far = 2 - 2 * upper
-    is_inner = (z == 1) | (z == 2)
-
-    @pl.when(is_inner)
-    def _():
-        for i in range(2):
-            block = place(1, far + i)
-            landed(block, second_recv.at[i])
-            remote(block, block, pass_send.at[i], pass_recv.at[i], f, near).start()
-
-    go(sendbuf.at[2], place(0, z), s_send.at[2], first_recv.at[z], f, inner)
+    far_outer(1)
+    hand_on(0)
 
     for m in range(mats):
         fpart[m] = jnp.dot(obuf[m].T, summed[m // kinds, m % kinds], preferred_element_type=jnp.float32)
@@ -341,6 +363,10 @@
             for k in range(kinds):
                 fsend[j - 1, c * kinds + k] = fchunk[expert * kinds + k].astype(jnp.bfloat16)
         go(fsend.at[j - 1], lowbuf.at[:, at, here], fz_send.at[j - 1], fz_recv.at[j - 1], f, d)
+    hand_on(1)
+    far_inner(0)
+    near_first(1)
+    far_inner(1)
     for c in range(CAP):
         expert = sel_ref[z * CAP + c]
         for k in range(kinds):
@@ -366,32 +392,43 @@
         for k in range(kinds):
             low_out[c * kinds + k] = obuf[expert * kinds + k]
 
-    def keep(c, source, sem):
-        block = place(c, source)
+    kept = []
+
+    def keep(c, source, k):
         there = pl.ds(pl.multiple_of(source * columns, columns), columns)
-        pltpu.make_async_copy(block, got_out.at[pl.ds(c * kinds, kinds), :, there], out_sem.at[sem]).start()
-
-    keep(0, z, 0)
-    keep(1, z, 1)
-    landed(place(1, near), near_recv)
-    keep(1, near, 2)
-    for n, source in enumerate((near, far, far + 1)):
-        landed(place(0, source), first_recv.at[source])
-        keep(0, source, 3 + n)
+        copy = pltpu.make_async_copy(
+            place(c, source, k), got_out.at[c * kinds + k, :, there], out_sem.at[len(kept)]
+        )
+        copy.start()
+        kept.append(copy)
+
+    for k in range(kinds):
+        keep(0, z, k)
+        keep(1, z, k)
+    for k in range(kinds):
+        landed(place(1, near, k), near_recv.at[k])
+        keep(1, near, k)
+    for k in range(kinds):
+        for source in (near, far, far + 1):
+            landed(place(0, source, k), first_recv.at[source, k])
+            keep(0, source, k)
 
     @pl.when(is_inner)
     def _():
         for i in range(2):
-            block = place(1, far + i)
-            remote(block, block, pass_send.at[i], pass_recv.at[i], f, near).wait_send()
+            for k in range(kinds):
+                block = place(1, far + i, k)
+                remote(block, block, pass_send.at[i, k], pass_recv.at[i, k], f, near).wait_send()
 
     @pl.when(jnp.logical_not(is_inner))
     def _():
         for i in range(2):
-            landed(place(1, far + i), pass_recv.at[i])
+            for k in range(kinds):
+                landed(place(1, far + i, k), pass_recv.at[i, k])
 
     for i in range(2):
-        keep(1, far + i, 6 + i)
+        for k in range(kinds):
+            keep(1, far + i, k)
     for buffer, recv in ((lowbuf, low_recv), (rightbuf, right_recv)):
         for j in range(1, shards_f):
             source = lax.rem(f + shards_f - j, shards_f)
@@ -401,13 +438,8 @@
     right_out[...] = rightbuf[...]
     for copy in started:
         copy.wait_send()
-    for n, (c, source) in enumerate(
-        ((0, z), (1, z), (1, near), (0, near), (0, far), (0, far + 1), (1, far), (1, far + 1))
-    ):
-        there = pl.ds(pl.multiple_of(source * columns, columns), columns)
-        pltpu.make_async_copy(
-            place(c, source), got_out.at[pl.ds(c * kinds, kinds), :, there], out_sem.at[n]
-        ).wait()
+    for copy in kept:
+        copy.wait()
 
 
 def fresh_kernel(used_ref, got_ref, low_ref, fact_ref, state_ref, left_ref):
@@ -501,7 +533,8 @@
             dma((near_z,)), dma((near_z,)),
             dma((near_f,)), dma((near_f,)),
             dma((near_f,)), dma((near_f,)),
-            dma((5,)), dma((groups,)), dma, dma((2,)), dma((2,)), dma((2,)), dma((8,)),
+            dma((5, kinds)), dma((groups, kinds)), dma((kinds,)),
+            dma((2, kinds)), dma((2, kinds)), dma((2, kinds)), dma((groups * mats,)),
         ],
         compiler_params=pltpu.CompilerParams(
             collective_id=0, has_side_effects=True, vmem_limit_bytes=VMEM_BYTES

time: 237 us -> 212 us (0.89)
  Pallas kernels: 230 us -> 205 us
    pallas_call x1, Pallas kernels: 220 us -> 195 us  [shards(): pl.pallas_call(functools.partial(step_kernel, shards_f, groups), out_shap...]
where the time goes in v3:
time: 212 us; the launch traced here: 210 us
  Pallas kernels  205 us (97%)
  other arithmetic  3.16 us (1%)
    pallas_call x1, Pallas kernels, shards(): pl.pallas_call(functools.partial(step_kernel, shards_f, groups), out_shap...  195 us
    pallas_call x1, Pallas kernels, shards(): pl.pallas_call(fresh_kernel, grid=(mats, rows // band), out_shape=(shape(...  10.2 us

profile of v3, /device:TPU:0, one launch (start us, length us, event | category | flops | bytes accessed | tf_op | source)
XLA Modules:
  0.0 210.2 jit_solution(7586523232684336980)
XLA Ops:
  0.6 0.9 convert_reduce_fusion.2
  1.6 0.7 multiply_add_fusion
  2.2 0.6 convert_reduce_fusion.1.used_ref
  2.8 0.1 select_reduce_fusion
  2.9 0.1 reshape.46
  3.0 0.1 reshape.45
  3.1 0.2 multiply_reduce_fusion
  3.3 0.1 mul.20
  3.3 0.1 reduce_sum.49
  3.5 0.6 pad_add_fusion.sel_ref
  4.1 194.6 %step.1 = (bf16[4,512,1536]{2,1,0:T(8,128)(2,1)}, bf16[4,512,128]{2,1,0:T(8,128)(2,1)}, bf16[4,128,1536]{2,1,0:T(8,128)(2,1)}, f32[6,128,384]{2,1,0:T(8,128)}) custom-call(s32[10]{0:T(128)} %pad_add_fusion.sel_ref, bf16[3,2,512,384]{3,2,1,0:T(8,128)(2,1)} %m_ref.1, bf16[3,2,512,384]{3,2,1,0:T(8,128)(2,1)} %g_ref.1, bf16[6,384,128]{2,1,0:T(8,128)(2,1)} %bitcast.7), custom_call_target="tpu_custom_call" | custom-call | tf_op jit(solution)/shard_map/step/pallas_call | solution.py:486
  198.6 0.0 copy-start
  198.6 10.2 %fresh.1 = (bf16[4,512,1536]{2,1,0:T(8,128)(2,1)}, f32[4,512,128]{2,1,0:T(8,128)}) custom-call(s32[4]{0:T(128)} %convert_reduce_fusion.1.used_ref, bf16[4,512,1536]{2,1,0:T(8,128)(2,1)} %get-tuple-element.9.got_ref, bf16[4,512,128]{2,1,0:T(8,128)(2,1)} %get-tuple-element.10.low_ref, bf16[4,128,1536]{2,1,0:T(8,128)(2,1)} %get-tuple-element.11.fact_ref), custom_call_target="tpu_custom_call" | custom-call | tf_op jit(solution)/shard_map/fresh/pallas_call | solution.py:546
  208.8 0.0 copy-done
  208.8 1.4 copy.9
  (1 shorter events, 0.0 us)
Async XLA Ops:
  198.6 10.2 %copy-start = (f32[6,128,384]{2,1,0:T(8,128)S(1)}, f32[6,128,384]{2,1,0:T(8,128)}, u32[]{:S(2)}) copy-start(f32[6,128,384]{2,1,0:T(8,128)} %get-tuple-element.14) | copy-start | bytes 3538948

commit v4 on v3

--- a/solution.py
+++ b/solution.py
@@ -141,28 +141,28 @@
 
 
 def step_kernel(
-    shards_f, groups,
+    shards_f, groups, kinds,
     sel_ref, m_ref, g_ref, r_ref,
     got_out, low_out, fact_out, right_out,
     summed, sendbuf, got, pbuf, precv, pchunk,
-    gram, gpair, ghalf, gchip, gpiece, gdepth, gfull, aug, wfull,
+    gram, gnear, gpair, ghalf, gchip, aug, wfull,
     obuf, fpart, fpair, fhalf, fchip, fchunk, fsend, lowbuf, sqbuf, sqrecv, rightbuf,
-    p_send, p_recv, ga_send, ga_recv, gb_send, gb_recv, gc_send, gc_recv, gd_send, gd_recv,
+    p_send, p_recv, ga_send, ga_recv, gb_send, gb_recv,
     w_send, w_recv, o_send, o_recv, fa_send, fa_recv, fb_send, fb_recv, fz_send, fz_recv,
     sq_send, sq_recv, low_send, low_recv, right_send, right_recv,
     s_send, first_recv, near_recv, second_recv, pass_send, pass_recv, out_sem,
 ):
-    experts, kinds, rows, columns = m_ref.shape
-    mats = experts * kinds
+    mats, rows, columns = m_ref.shape
+    experts = mats // kinds
     slots = CAP * kinds
     rank = r_ref.shape[-1]
-    half_m = mats // 2
+    units = 2 * mats // groups
     f, z = greet(shards_f, groups)
     core = lax.rem(f, 2)
     chip = f // 2
     chips = shards_f // 2
     pair = chip * 2 + 1 - core
-    zrows = rows // groups
+    urows = rows // 2
     started = []
 
     def go(src, dst, send_sem, recv_sem, to_f, to_z):
@@ -174,28 +174,26 @@
     def landed(dst, recv_sem):
         remote(dst, dst, recv_sem, recv_sem, f, z).wait_recv()
 
+    for j in (2, 3, 1, 0):
+        d = lax.rem(z + j, groups)
+        for i in range(units):
+            u = d * units + i
+            m = u // 2
+            top = lax.rem(u, 2) * urows
+
+            @pl.loop(0, urows // 128)
+            def _(b):
+                at = pl.ds(pl.multiple_of(top + b * 128, 128), 128)
+                total = m_ref[m, at, :].astype(jnp.float32) + g_ref[m, at, :].astype(jnp.float32)
+                low = total.astype(jnp.bfloat16)
+                summed[m, at, :] = low
+                pbuf[u, pl.ds(pl.multiple_of(b * 128, 128), 128), :] = jnp.dot(
+                    low, r_ref[m], preferred_element_type=jnp.float32
+                )
+        if j:
+            go(pbuf.at[pl.ds(d * units, units)], precv.at[j - 1], p_send.at[j - 1], p_recv.at[j - 1], f, d)
+
     step = 128
-    zmine = pl.ds(pl.multiple_of(z * zrows, zrows), zrows)
-    for e in range(experts):
-        for k in range(kinds):
-            @pl.loop(0, rows // step)
-            def _(i):
-                at = pl.ds(pl.multiple_of(i * step, step), step)
-                total = m_ref[e, k, at, :].astype(jnp.float32) + g_ref[e, k, at, :].astype(jnp.float32)
-                low = total.astype(jnp.bfloat16)
-                summed[e, k, at, :] = low
-                pbuf[e * kinds + k, at, :] = jnp.dot(low, r_ref[e * kinds + k], preferred_element_type=jnp.float32)
-        for j in (2, 3, 1):
-            d = lax.rem(z + j, groups)
-            go(
-                pbuf.at[pl.ds(e * kinds, kinds), pl.ds(pl.multiple_of(d * zrows, zrows), zrows), :],
-                precv.at[j - 1, pl.ds(e * kinds, kinds)],
-                p_send.at[j - 1, e],
-                p_recv.at[j - 1, e],
-                f,
-                d,
-            )
-
     near = z + 1 - 2 * lax.rem(z, 2)
     upper = z // 2
     inner = 2 - upper
@@ -212,7 +210,7 @@
             @pl.loop(0, rows // step)
             def _(i):
                 at = pl.ds(pl.multiple_of(i * step, step), step)
-                sendbuf[unit, k, at, :] = summed[expert, k, at, :]
+                sendbuf[unit, k, at, :] = summed[expert * kinds + k, at, :]
     here = pl.ds(pl.multiple_of(z * columns, columns), columns)
     for c in range(CAP):
         expert = sel_ref[z * CAP + c]
@@ -220,7 +218,7 @@
             @pl.loop(0, rows // step)
             def _(i):
                 at = pl.ds(pl.multiple_of(i * step, step), step)
-                got[c * kinds + k, at, here] = summed[expert, k, at, :]
+                got[c * kinds + k, at, here] = summed[expert * kinds + k, at, :]
 
     def place(c, source, k):
         return got.at[c * kinds + k, :, pl.ds(pl.multiple_of(source * columns, columns), columns)]
@@ -254,78 +252,69 @@
                 landed(block, second_recv.at[i, k])
                 remote(block, block, pass_send.at[i, k], pass_recv.at[i, k], f, near).start()
 
+    odd = lax.rem(z, 2)
     for j in range(1, groups):
-        for e in range(experts):
-            landed(precv.at[j - 1, pl.ds(e * kinds, kinds)], p_recv.at[j - 1, e])
+        landed(precv.at[j - 1], p_recv.at[j - 1])
+    for i in range(units):
+        total = pbuf[z * units + i]
+        for j in range(1, groups):
+            total = total + precv[j - 1, i]
+        pchunk[i] = total
+
+    def gram_of(i):
+        panel = pchunk[i]
+        return jnp.dot(panel.T, panel, precision=HIGHEST, preferred_element_type=jnp.float32)
+
+    gram[2] = gram_of(2 - 2 * odd)
+    shared = go(gram.at[2], gnear, ga_send.at[0], ga_recv.at[0], f, near)
+    gram[0] = gram_of(odd) + gram_of(odd + 1)
+    shared.wait_recv()
+    gram[1] = gram[2] + gnear[...]
     far_second(0)
     near_second(0)
-
-    for m in range(mats):
-        total = pbuf[m, zmine, :]
-        for j in range(1, groups):
-            total = total + precv[j - 1, m]
-        pchunk[m] = total
-        gram[m] = jnp.dot(total.T, total, precision=HIGHEST, preferred_element_type=jnp.float32)
-    go(gram.at[pl.ds((1 - core) * half_m, half_m)], gpair, ga_send, ga_recv, pair, z).wait_recv()
-    ghalf[...] = gram[pl.ds(core * half_m, half_m)] + gpair[...]
-    prows = rank // chips
-    cmine = pl.ds(pl.multiple_of(chip * prows, prows), prows)
+    far_second(1)
+    near_second(1)
+    near_first(0)
+    near_first(1)
+    go(gram.at[1 - core], gpair, ga_send.at[1], ga_recv.at[1], pair, z).wait_recv()
+    total = gram[core] + gpair[...]
+    ghalf[...] = total
     for j in (2, 1, 3):
-        other = lax.rem(chip + j, chips)
         go(
-            ghalf.at[:, pl.ds(pl.multiple_of(other * prows, prows), prows), :],
-            gchip.at[j - 1], gb_send.at[j - 1], gb_recv.at[j - 1], other * 2 + core, z,
+            ghalf, gchip.at[j - 1], gb_send.at[j - 1], gb_recv.at[j - 1],
+            lax.rem(chip + j, chips) * 2 + core, z,
         )
-    total = ghalf[:, cmine, :]
     for j in range(1, chips):
         landed(gchip.at[j - 1], gb_recv.at[j - 1])
         total = total + gchip[j - 1]
-    gpiece[...] = total
-    for j in (2, 3, 1):
-        go(gpiece, gdepth.at[j - 1], gc_send.at[j - 1], gc_recv.at[j - 1], f, lax.rem(z + j, groups))
-    for j in range(1, groups):
-        landed(gdepth.at[j - 1], gc_recv.at[j - 1])
-        total = total + gdepth[j - 1]
-    gfull[:, cmine, :] = total
-    for j in (2, 1, 3):
-        part = gfull.at[:, cmine, :]
-        go(part, part, gd_send.at[j - 1], gd_recv.at[j - 1], lax.rem(chip + j, chips) * 2 + core, z)
-    for j in range(1, chips):
-        other = lax.rem(chip + chips - j, chips)
-        landed(gfull.at[:, pl.ds(pl.multiple_of(other * prows, prows), prows), :], gd_recv.at[j - 1])
-
-    far_second(1)
-    far_outer(0)
-    near_second(1)
-    near_first(0)
 
     row_at = lax.broadcasted_iota(jnp.int32, (rank, rank), 0)
     col_at = lax.broadcasted_iota(jnp.int32, (rank, rank), 1)
     eye = (row_at == col_at).astype(jnp.float32)
-    for m in range(half_m):
-        aug[m, :, :rank] = gfull[m] + ridge_term * eye
-        aug[m, :, rank:] = eye
-    inverse_factor(aug, half_m, rank)
-    wmine = pl.ds(core * half_m, half_m)
-    wfull[wmine] = aug[:, :, rank:]
-    go(wfull.at[wmine], wfull.at[wmine], w_send, w_recv, pair, z)
-    landed(wfull.at[pl.ds((1 - core) * half_m, half_m)], w_recv)
-
-    for m in range(mats):
-        ortho = jnp.dot(pchunk[m], wfull[m].T, precision=HIGHEST, preferred_element_type=jnp.float32)
-        obuf[m, zmine, :] = ortho.astype(jnp.bfloat16)
+    aug[0, :, :rank] = total + ridge_term * eye
+    aug[0, :, rank:] = eye
+    inverse_factor(aug, 1, rank)
+    wfull[core] = aug[0, :, rank:]
+    go(wfull.at[core], wfull.at[core], w_send, w_recv, pair, z)
+    landed(wfull.at[1 - core], w_recv)
+
+    for i, which in enumerate((odd, 0, 1 - odd)):
+        ortho = jnp.dot(pchunk[i], wfull[which].T, precision=HIGHEST, preferred_element_type=jnp.float32)
+        obuf[z * units + i] = ortho.astype(jnp.bfloat16)
     for j in (2, 3, 1):
-        part = obuf.at[:, zmine, :]
+        part = obuf.at[pl.ds(z * units, units)]
         go(part, part, o_send.at[j - 1], o_recv.at[j - 1], f, lax.rem(z + j, groups))
     for j in range(1, groups):
         source = lax.rem(z + groups - j, groups)
-        landed(obuf.at[:, pl.ds(pl.multiple_of(source * zrows, zrows), zrows), :], o_recv.at[j - 1])
-
-    far_outer(1)
+        landed(obuf.at[pl.ds(source * units, units)], o_recv.at[j - 1])
+
+    far_inner(0)
     hand_on(0)
 
     for m in range(mats):
-        fpart[m] = jnp.dot(obuf[m].T, summed[m // kinds, m % kinds], preferred_element_type=jnp.float32)
+        fpart[m] = jnp.dot(
+            obuf[2 * m].T, summed[m, :urows], preferred_element_type=jnp.float32
+        ) + jnp.dot(obuf[2 * m + 1].T, summed[m, urows:], preferred_element_type=jnp.float32)
         low_rows = rank // 2
         go(
             fpart.at[m, pl.ds(pl.multiple_of((1 - core) * low_rows, low_rows), low_rows), :],
@@ -364,8 +353,8 @@
                 fsend[j - 1, c * kinds + k] = fchunk[expert * kinds + k].astype(jnp.bfloat16)
         go(fsend.at[j - 1], lowbuf.at[:, at, here], fz_send.at[j - 1], fz_recv.at[j - 1], f, d)
     hand_on(1)
-    far_inner(0)
-    near_first(1)
+    far_outer(0)
+    far_outer(1)
     far_inner(1)
     for c in range(CAP):
         expert = sel_ref[z * CAP + c]
@@ -375,22 +364,30 @@
         source = lax.rem(z + groups - j, groups)
         there = pl.ds(pl.multiple_of(source * columns, columns), columns)
         landed(lowbuf.at[:, at, there], fz_recv.at[j - 1])
-    for j in range(1, shards_f):
+    for j in (2, 1, 3):
         part = lowbuf.at[:, at, :]
-        go(part, part, low_send.at[j - 1], low_recv.at[j - 1], lax.rem(f + j, shards_f), z)
+        go(part, part, low_send.at[j - 1], low_recv.at[j - 1], lax.rem(chip + j, chips) * 2 + core, z)
     square = sqbuf[...]
     for j in range(1, groups):
         landed(sqrecv.at[j - 1], sq_recv.at[j - 1])
         square = square + sqrecv[j - 1]
     mean_square = jnp.sum(square, axis=2, keepdims=True) / (groups * columns)
     rightbuf[:, at, :] = fchunk[...] * lax.rsqrt(mean_square + epsilon)
-    for j in range(1, shards_f):
+    for j in (2, 1, 3):
         part = rightbuf.at[:, at, :]
-        go(part, part, right_send.at[j - 1], right_recv.at[j - 1], lax.rem(f + j, shards_f), z)
+        go(part, part, right_send.at[j - 1], right_recv.at[j - 1], lax.rem(chip + j, chips) * 2 + core, z)
+    theirs = pl.ds(pl.multiple_of((1 - core) * low_rows, low_rows), low_rows)
+    for buffer, sent, recv in ((lowbuf, low_send, low_recv), (rightbuf, right_send, right_recv)):
+        for j in range(1, chips):
+            start = core * low_rows + lax.rem(chip + chips - j, chips) * piece
+            landed(buffer.at[:, pl.ds(pl.multiple_of(start, piece), piece), :], recv.at[j - 1])
+        part = buffer.at[:, own, :]
+        go(part, part, sent.at[chips - 1], recv.at[chips - 1], pair, z)
     for c in range(CAP):
         expert = sel_ref[z * CAP + c]
         for k in range(kinds):
-            low_out[c * kinds + k] = obuf[expert * kinds + k]
+            low_out[c * kinds + k, :urows] = obuf[(expert * kinds + k) * 2]
+            low_out[c * kinds + k, urows:] = obuf[(expert * kinds + k) * 2 + 1]
 
     kept = []
 
@@ -430,10 +427,7 @@
         for k in range(kinds):
             keep(1, far + i, k)
     for buffer, recv in ((lowbuf, low_recv), (rightbuf, right_recv)):
-        for j in range(1, shards_f):
-            source = lax.rem(f + shards_f - j, shards_f)
-            start = lax.rem(source, 2) * low_rows + (source // 2) * piece
-            landed(buffer.at[:, pl.ds(pl.multiple_of(start, piece), piece), :], recv.at[j - 1])
+        landed(buffer.at[:, theirs, :], recv.at[chips - 1])
     fact_out[...] = lowbuf[...]
     right_out[...] = rightbuf[...]
     for copy in started:
@@ -479,12 +473,11 @@
     dma = pltpu.SemaphoreType.DMA
     chips = shards_f // 2
     every = experts * kinds
-    half_m = every // 2
-    zrows = rows // groups
+    units = 2 * every // groups
     piece = rank // shards_f
-    near_z, near_c, near_f = groups - 1, chips - 1, shards_f - 1
+    near_z, near_c = groups - 1, chips - 1
     got, low, fact, right = pl.pallas_call(
-        functools.partial(step_kernel, shards_f, groups),
+        functools.partial(step_kernel, shards_f, groups, kinds),
         out_shape=(
             shape((mats, rows, hidden), bf16),
             shape((mats, rows, rank), bf16),
@@ -494,22 +487,20 @@
         in_specs=[smem, vmem, vmem, vmem],
         out_specs=(hbm, vmem, vmem, vmem),
         scratch_shapes=[
-            pltpu.VMEM((experts, kinds, rows, columns), bf16),
+            pltpu.VMEM((every, rows, columns), bf16),
             pltpu.VMEM((5, kinds, rows, columns), bf16),
             pltpu.VMEM((mats, rows, hidden), bf16),
-            pltpu.VMEM((every, rows, rank), f32),
-            pltpu.VMEM((near_z, every, zrows, rank), f32),
-            pltpu.VMEM((every, zrows, rank), f32),
-            pltpu.VMEM((every, rank, rank), f32),
-            pltpu.VMEM((half_m, rank, rank), f32),
-            pltpu.VMEM((half_m, rank, rank), f32),
-            pltpu.VMEM((near_c, half_m, rank // chips, rank), f32),
-            pltpu.VMEM((half_m, rank // chips, rank), f32),
-            pltpu.VMEM((near_z, half_m, rank // chips, rank), f32),
-            pltpu.VMEM((half_m, rank, rank), f32),
-            pltpu.VMEM((half_m, rank, 2 * rank), f32),
-            pltpu.VMEM((every, rank, rank), f32),
-            pltpu.VMEM((every, rows, rank), bf16),
+            pltpu.VMEM((2 * every, rows // 2, rank), f32),
+            pltpu.VMEM((near_z, units, rows // 2, rank), f32),
+            pltpu.VMEM((units, rows // 2, rank), f32),
+            pltpu.VMEM((3, rank, rank), f32),
+            pltpu.VMEM((rank, rank), f32),
+            pltpu.VMEM((rank, rank), f32),
+            pltpu.VMEM((rank, rank), f32),
+            pltpu.VMEM((near_c, rank, rank), f32),
+            pltpu.VMEM((1, rank, 2 * rank), f32),
+            pltpu.VMEM((2, rank, rank), f32),
+            pltpu.VMEM((2 * every, rows // 2, rank), bf16),
             pltpu.VMEM((every, rank, columns), f32),
             pltpu.VMEM((every, rank // 2, columns), f32),
             pltpu.VMEM((every, rank // 2, columns), f32),
@@ -520,10 +511,8 @@
             pltpu.VMEM((every, piece, 128), f32),
             pltpu.VMEM((near_z, every, piece, 128), f32),
             pltpu.VMEM((every, rank, columns), f32),
-            dma((near_z, experts)), dma((near_z, experts)),
-            dma, dma,
-            dma((near_c,)), dma((near_c,)),
             dma((near_z,)), dma((near_z,)),
+            dma((2,)), dma((2,)),
             dma((near_c,)), dma((near_c,)),
             dma, dma,
             dma((near_z,)), dma((near_z,)),
@@ -531,8 +520,8 @@
             dma((near_c,)), dma((near_c,)),
             dma((near_z,)), dma((near_z,)),
             dma((near_z,)), dma((near_z,)),
-            dma((near_f,)), dma((near_f,)),
-            dma((near_f,)), dma((near_f,)),
+            dma((chips,)), dma((chips,)),
+            dma((chips,)), dma((chips,)),
             dma((5, kinds)), dma((groups, kinds)), dma((kinds,)),
             dma((2, kinds)), dma((2, kinds)), dma((2, kinds)), dma((groups * mats,)),
         ],
@@ -540,7 +529,12 @@
             collective_id=0, has_side_effects=True, vmem_limit_bytes=VMEM_BYTES
         ),
         name="step",
-    )(sel, momentum, gradient, right_in.reshape(every, columns, rank))
+    )(
+        sel,
+        momentum.reshape(every, rows, columns),
+        gradient.reshape(every, rows, columns),
+        right_in.reshape(every, columns, rank),
+    )
 
     band = min(rows, 256)
     state, left = pl.pallas_call(

time: 212 us -> 207 us (0.976)
  Pallas kernels: 205 us -> 201 us
    pallas_call x1, Pallas kernels: 195 us -> 191 us  [shards(): pl.pallas_call(functools.partial(step_kernel, shards_f, groups, kinds), o...]
where the time goes in v4:
time: 207 us; the launch traced here: 206 us
  Pallas kernels  201 us (97%)
  other arithmetic  3.16 us (2%)
    pallas_call x1, Pallas kernels, shards(): pl.pallas_call(functools.partial(step_kernel, shards_f, groups, kinds), o...  191 us
    pallas_call x1, Pallas kernels, shards(): pl.pallas_call(fresh_kernel, grid=(mats, rows // band), out_shape=(shape(...  10.2 us

profile of v4, /device:TPU:0, one launch (start us, length us, event | category | flops | bytes accessed | tf_op | source)
XLA Modules:
  0.0 206.4 jit_solution(11124963988903628252)
XLA Ops:
  0.6 0.9 convert_reduce_fusion.2
  1.6 0.7 multiply_add_fusion
  2.2 0.6 convert_reduce_fusion.1.used_ref
  2.8 0.1 select_reduce_fusion
  2.9 0.1 reshape.52
  3.0 0.1 reshape.51
  3.1 0.2 multiply_reduce_fusion
  3.3 0.1 mul.20
  3.3 0.1 reduce_sum.49
  3.5 0.6 pad_add_fusion.sel_ref
  4.1 190.8 %step.1 = (bf16[4,512,1536]{2,1,0:T(8,128)(2,1)}, bf16[4,512,128]{2,1,0:T(8,128)(2,1)}, bf16[4,128,1536]{2,1,0:T(8,128)(2,1)}, f32[6,128,384]{2,1,0:T(8,128)}) custom-call(s32[10]{0:T(128)} %pad_add_fusion.sel_ref, bf16[6,512,384]{2,1,0:T(8,128)(2,1)} %bitcast.8, bf16[6,512,384]{2,1,0:T(8,128)(2,1)} %bitcast.9, bf16[6,384,128]{2,1,0:T(8,128)(2,1)} %bitcast.11), custom_call_target="tpu_custom_call" | custom-call | tf_op jit(solution)/shard_map/step/pallas_call | solution.py:479
  194.8 0.0 copy-start
  194.9 10.2 %fresh.1 = (bf16[4,512,1536]{2,1,0:T(8,128)(2,1)}, f32[4,512,128]{2,1,0:T(8,128)}) custom-call(s32[4]{0:T(128)} %convert_reduce_fusion.1.used_ref, bf16[4,512,1536]{2,1,0:T(8,128)(2,1)} %get-tuple-element.9.got_ref, bf16[4,512,128]{2,1,0:T(8,128)(2,1)} %get-tuple-element.10.low_ref, bf16[4,128,1536]{2,1,0:T(8,128)(2,1)} %get-tuple-element.11.fact_ref), custom_call_target="tpu_custom_call" | custom-call | tf_op jit(solution)/shard_map/fresh/pallas_call | solution.py:540
  205.0 0.0 copy-done
  205.0 1.4 copy.9
  (1 shorter events, 0.0 us)
Async XLA Ops:
  194.8 10.2 %copy-start = (f32[6,128,384]{2,1,0:T(8,128)S(1)}, f32[6,128,384]{2,1,0:T(8,128)}, u32[]{:S(2)}) copy-start(f32[6,128,384]{2,1,0:T(8,128)} %get-tuple-element.14) | copy-start | bytes 3538948

commit v5 on v4

--- a/solution.py
+++ b/solution.py
@@ -142,13 +142,13 @@
 
 def step_kernel(
     shards_f, groups, kinds,
-    sel_ref, m_ref, g_ref, r_ref,
+    own_ref, m_ref, g_ref, r_ref,
     got_out, low_out, fact_out, right_out,
-    summed, sendbuf, got, pbuf, precv, pchunk,
+    summed, sendbuf, got, pbuf, prelay, pjoin, pnear, pfar, pchunk,
     gram, gnear, gpair, ghalf, gchip, aug, wfull,
     obuf, fpart, fpair, fhalf, fchip, fchunk, fsend, lowbuf, sqbuf, sqrecv, rightbuf,
-    p_send, p_recv, ga_send, ga_recv, gb_send, gb_recv,
-    w_send, w_recv, o_send, o_recv, fa_send, fa_recv, fb_send, fb_recv, fz_send, fz_recv,
+    p_send, p_recv, r_send, r_recv, x_send, x_recv, ga_send, ga_recv, gb_send, gb_recv,
+    w_send, w_recv, o_send, o_recv, op_send, op_recv, fa_send, fa_recv, fb_send, fb_recv, fz_send, fz_recv,
     sq_send, sq_recv, low_send, low_recv, right_send, right_recv,
     s_send, first_recv, near_recv, second_recv, pass_send, pass_recv, out_sem,
 ):
@@ -174,8 +174,21 @@
     def landed(dst, recv_sem):
         remote(dst, dst, recv_sem, recv_sem, f, z).wait_recv()
 
-    for j in (2, 3, 1, 0):
-        d = lax.rem(z + j, groups)
+    near = z + 1 - 2 * lax.rem(z, 2)
+    upper = z // 2
+    inner = 2 - upper
+    outer = 3 - 3 * upper
+    far = 2 - 2 * upper
+    is_inner = (z == 1) | (z == 2)
+    is_outer = jnp.logical_not(is_inner)
+
+    def relay(t, i, u):
+        return remote(pbuf.at[u], prelay.at[t, i], r_send.at[t, i], r_recv.at[t, i], f, near)
+
+    def across(t, i, d):
+        return remote(pjoin.at[t, i], pfar.at[i], x_send.at[t, i], x_recv.at[i], f, d)
+
+    for t, d in enumerate((outer, inner, near, z)):
         for i in range(units):
             u = d * units + i
             m = u // 2
@@ -190,21 +203,34 @@
                 pbuf[u, pl.ds(pl.multiple_of(b * 128, 128), 128), :] = jnp.dot(
                     low, r_ref[m], preferred_element_type=jnp.float32
                 )
-        if j:
-            go(pbuf.at[pl.ds(d * units, units)], precv.at[j - 1], p_send.at[j - 1], p_recv.at[j - 1], f, d)
+
+            if t < 2:
+                @pl.when(is_outer)
+                def _():
+                    relay(t, i, u).start()
+
+        if t == 2:
+            go(pbuf.at[pl.ds(near * units, units)], pnear, p_send, p_recv, f, near)
+
+    @pl.when(is_inner)
+    def _():
+        for t, d in enumerate((outer, inner)):
+            for i in range(units):
+                landed(prelay.at[t, i], r_recv.at[t, i])
+                pjoin[t, i] = pbuf[d * units + i] + prelay[t, i]
+                across(t, i, d).start()
 
     step = 128
-    near = z + 1 - 2 * lax.rem(z, 2)
-    upper = z // 2
-    inner = 2 - upper
-    outer = 3 - 3 * upper
-    picks = (
-        sel_ref[groups * CAP + 1 - upper],
-        sel_ref[outer * CAP],
-        sel_ref[inner * CAP],
-        sel_ref[near * CAP],
-        sel_ref[near * CAP + 1],
-    )
+    owner = [own_ref[e] for e in range(experts)]
+    position = [sum(((owner[b] == owner[e]).astype(jnp.int32) for b in range(e)), jnp.int32(0)) for e in range(experts)]
+
+    def taken(d, c):
+        return sum((jnp.where((owner[e] == d) & (position[e] == c), e, 0) for e in range(experts)), jnp.int32(0))
+
+    second = sum(
+        (jnp.where((owner[e] // 2 == 1 - upper) & (position[e] == 1), e, 0) for e in range(experts)), jnp.int32(0)
+    )
+    picks = (second, taken(outer, 0), taken(inner, 0), taken(near, 0), taken(near, 1))
     for unit, expert in enumerate(picks):
         for k in range(kinds):
             @pl.loop(0, rows // step)
@@ -213,7 +239,7 @@
                 sendbuf[unit, k, at, :] = summed[expert * kinds + k, at, :]
     here = pl.ds(pl.multiple_of(z * columns, columns), columns)
     for c in range(CAP):
-        expert = sel_ref[z * CAP + c]
+        expert = taken(z, c)
         for k in range(kinds):
             @pl.loop(0, rows // step)
             def _(i):
@@ -240,9 +266,6 @@
 
     def near_second(k):
         send(4, 1, near_recv.at[k], near, k)
-
-    far = 2 - 2 * upper
-    is_inner = (z == 1) | (z == 2)
 
     def hand_on(k):
         @pl.when(is_inner)
@@ -253,13 +276,10 @@
                 remote(block, block, pass_send.at[i, k], pass_recv.at[i, k], f, near).start()
 
     odd = lax.rem(z, 2)
-    for j in range(1, groups):
-        landed(precv.at[j - 1], p_recv.at[j - 1])
+    landed(pnear, p_recv)
     for i in range(units):
-        total = pbuf[z * units + i]
-        for j in range(1, groups):
-            total = total + precv[j - 1, i]
-        pchunk[i] = total
+        landed(pfar.at[i], x_recv.at[i])
+        pchunk[i] = pbuf[z * units + i] + pnear[i] + pfar[i]
 
     def gram_of(i):
         panel = pchunk[i]
@@ -276,6 +296,7 @@
     near_second(1)
     near_first(0)
     near_first(1)
+    far_outer(0)
     go(gram.at[1 - core], gpair, ga_send.at[1], ga_recv.at[1], pair, z).wait_recv()
     total = gram[core] + gpair[...]
     ghalf[...] = total
@@ -301,12 +322,28 @@
     for i, which in enumerate((odd, 0, 1 - odd)):
         ortho = jnp.dot(pchunk[i], wfull[which].T, precision=HIGHEST, preferred_element_type=jnp.float32)
         obuf[z * units + i] = ortho.astype(jnp.bfloat16)
-    for j in (2, 3, 1):
-        part = obuf.at[pl.ds(z * units, units)]
-        go(part, part, o_send.at[j - 1], o_recv.at[j - 1], f, lax.rem(z + j, groups))
-    for j in range(1, groups):
-        source = lax.rem(z + groups - j, groups)
-        landed(obuf.at[pl.ds(source * units, units)], o_recv.at[j - 1])
+    def chunk_of(source):
+        return obuf.at[pl.ds(source * units, units)]
+
+    def ortho_on(i):
+        part = chunk_of(far + i)
+        return remote(part, part, op_send.at[i], op_recv.at[i], f, near)
+
+    go(chunk_of(z), chunk_of(z), o_send.at[0], o_recv.at[lax.rem(z, 2)], f, inner)
+    go(chunk_of(z), chunk_of(z), o_send.at[1], o_recv.at[2], f, near)
+
+    @pl.when(is_inner)
+    def _():
+        for i in range(2):
+            landed(chunk_of(far + i), o_recv.at[i])
+            ortho_on(i).start()
+
+    landed(chunk_of(near), o_recv.at[2])
+
+    @pl.when(is_outer)
+    def _():
+        for i in range(2):
+            landed(chunk_of(far + i), op_recv.at[i])
 
     far_inner(0)
     hand_on(0)
@@ -348,16 +385,15 @@
     for j in (2, 3, 1):
         d = lax.rem(z + j, groups)
         for c in range(CAP):
-            expert = sel_ref[d * CAP + c]
+            expert = taken(d, c)
             for k in range(kinds):
                 fsend[j - 1, c * kinds + k] = fchunk[expert * kinds + k].astype(jnp.bfloat16)
         go(fsend.at[j - 1], lowbuf.at[:, at, here], fz_send.at[j - 1], fz_recv.at[j - 1], f, d)
     hand_on(1)
-    far_outer(0)
     far_outer(1)
     far_inner(1)
     for c in range(CAP):
-        expert = sel_ref[z * CAP + c]
+        expert = taken(z, c)
         for k in range(kinds):
             lowbuf[c * kinds + k, at, here] = fchunk[expert * kinds + k].astype(jnp.bfloat16)
     for j in range(1, groups):
@@ -384,7 +420,7 @@
         part = buffer.at[:, own, :]
         go(part, part, sent.at[chips - 1], recv.at[chips - 1], pair, z)
     for c in range(CAP):
-        expert = sel_ref[z * CAP + c]
+        expert = taken(z, c)
         for k in range(kinds):
             low_out[c * kinds + k, :urows] = obuf[(expert * kinds + k) * 2]
             low_out[c * kinds + k, urows:] = obuf[(expert * kinds + k) * 2 + 1]
@@ -416,9 +452,16 @@
             for k in range(kinds):
                 block = place(1, far + i, k)
                 remote(block, block, pass_send.at[i, k], pass_recv.at[i, k], f, near).wait_send()
-
-    @pl.when(jnp.logical_not(is_inner))
+            ortho_on(i).wait_send()
+        for t, d in enumerate((outer, inner)):
+            for i in range(units):
+                across(t, i, d).wait_send()
+
+    @pl.when(is_outer)
     def _():
+        for t, d in enumerate((outer, inner)):
+            for i in range(units):
+                relay(t, i, d * units + i).wait_send()
         for i in range(2):
             for k in range(kinds):
                 landed(place(1, far + i, k), pass_recv.at[i, k])
@@ -458,10 +501,6 @@
     earlier = index_line[None, :] < index_line[:, None]
     position = jnp.sum((same_owner & earlier).astype(jnp.int32), axis=1)
     slot = owners * CAP + position
-    hit = slot[:, None] == jnp.arange(groups * CAP, dtype=jnp.int32)[None, :]
-    sel = jnp.sum(jnp.where(hit, index_line[:, None], 0), axis=0).astype(jnp.int32)
-    second = sel.reshape(groups, CAP)[:, 1] * jnp.sum(hit, axis=0).reshape(groups, CAP)[:, 1]
-    sel = jnp.concatenate([sel, second.reshape(2, groups // 2).sum(axis=1).astype(jnp.int32)])
     here = slot[:, None] == (z * CAP + jnp.arange(mats, dtype=jnp.int32) // kinds)[None, :]
     used = jnp.sum(here.astype(jnp.int32), axis=0)
 
@@ -491,7 +530,10 @@
             pltpu.VMEM((5, kinds, rows, columns), bf16),
             pltpu.VMEM((mats, rows, hidden), bf16),
             pltpu.VMEM((2 * every, rows // 2, rank), f32),
-            pltpu.VMEM((near_z, units, rows // 2, rank), f32),
+            pltpu.VMEM((2, units, rows // 2, rank), f32),
+            pltpu.VMEM((2, units, rows // 2, rank), f32),
+            pltpu.VMEM((units, rows // 2, rank), f32),
+            pltpu.VMEM((units, rows // 2, rank), f32),
             pltpu.VMEM((units, rows // 2, rank), f32),
             pltpu.VMEM((3, rank, rank), f32),
             pltpu.VMEM((rank, rank), f32),
@@ -511,11 +553,13 @@
             pltpu.VMEM((every, piece, 128), f32),
             pltpu.VMEM((near_z, every, piece, 128), f32),
             pltpu.VMEM((every, rank, columns), f32),
-            dma((near_z,)), dma((near_z,)),
+            dma, dma,
+            dma((2, units)), dma((2, units)),
+            dma((2, units)), dma((units,)),
             dma((2,)), dma((2,)),
             dma((near_c,)), dma((near_c,)),
             dma, dma,
-            dma((near_z,)), dma((near_z,)),
+            dma((2,)), dma((3,)), dma((2,)), dma((2,)),
             dma((every,)), dma((every,)),
             dma((near_c,)), dma((near_c,)),
             dma((near_z,)), dma((near_z,)),
@@ -530,7 +574,7 @@
         ),
         name="step",
     )(
-        sel,
+        owners,
         momentum.reshape(every, rows, columns),
         gradient.reshape(every, rows, columns),
         right_in.reshape(every, columns, rank),

time: 207 us -> 183 us (0.88)
  Pallas kernels: 201 us -> 178 us
    pallas_call x1, Pallas kernels: 191 us -> 168 us  [shards(): pl.pallas_call(functools.partial(step_kernel, shards_f, groups, kinds), o...]
where the time goes in v5:
time: 183 us; the launch traced here: 182 us
  Pallas kernels  178 us (97%)
  other arithmetic  2.17 us (1%)
    pallas_call x1, Pallas kernels, shards(): pl.pallas_call(functools.partial(step_kernel, shards_f, groups, kinds), o...  168 us
    pallas_call x1, Pallas kernels, shards(): pl.pallas_call(fresh_kernel, grid=(mats, rows // band), out_shape=(shape(...  10.2 us

profile of v5, /device:TPU:0, one launch (start us, length us, event | category | flops | bytes accessed | tf_op | source)
XLA Modules:
  0.0 182.4 jit_solution(4346207446230189233)
XLA Ops:
  0.6 0.9 convert_reduce_fusion.1
  1.6 0.7 multiply_add_fusion
  2.2 0.6 convert_reduce_fusion.used_ref
  2.8 168.0 %step.1 = (bf16[4,512,1536]{2,1,0:T(8,128)(2,1)}, bf16[4,512,128]{2,1,0:T(8,128)(2,1)}, bf16[4,128,1536]{2,1,0:T(8,128)(2,1)}, f32[6,128,384]{2,1,0:T(8,128)}) custom-call(s32[3]{0:T(128)} %own_ref.1, bf16[6,512,384]{2,1,0:T(8,128)(2,1)} %bitcast.8, bf16[6,512,384]{2,1,0:T(8,128)(2,1)} %bitcast.9, bf16[6,384,128]{2,1,0:T(8,128)(2,1)} %bitcast.11), custom_call_target="tpu_custom_call" | custom-call | tf_op jit(solution)/shard_map/step/pallas_call | solution.py:518
  170.9 0.0 copy-start
  170.9 10.2 %fresh.1 = (bf16[4,512,1536]{2,1,0:T(8,128)(2,1)}, f32[4,512,128]{2,1,0:T(8,128)}) custom-call(s32[4]{0:T(128)} %convert_reduce_fusion.used_ref, bf16[4,512,1536]{2,1,0:T(8,128)(2,1)} %get-tuple-element.9.got_ref, bf16[4,512,128]{2,1,0:T(8,128)(2,1)} %get-tuple-element.10.low_ref, bf16[4,128,1536]{2,1,0:T(8,128)(2,1)} %get-tuple-element.11.fact_ref), custom_call_target="tpu_custom_call" | custom-call | tf_op jit(solution)/shard_map/fresh/pallas_call | solution.py:584
  181.0 0.0 copy-done
  181.0 1.4 copy.8
  (1 shorter events, 0.0 us)
Async XLA Ops:
  170.9 10.2 %copy-start = (f32[6,128,384]{2,1,0:T(8,128)S(1)}, f32[6,128,384]{2,1,0:T(8,128)}, u32[]{:S(2)}) copy-start(f32[6,128,384]{2,1,0:T(8,128)} %get-tuple-element.14) | copy-start | bytes 3538948

commit v6 on v5

--- a/solution.py
+++ b/solution.py
@@ -143,7 +143,7 @@
 def step_kernel(
     shards_f, groups, kinds,
     own_ref, m_ref, g_ref, r_ref,
-    got_out, low_out, fact_out, right_out,
+    state_out, left_out, right_out,
     summed, sendbuf, got, pbuf, prelay, pjoin, pnear, pfar, pchunk,
     gram, gnear, gpair, ghalf, gchip, aug, wfull,
     obuf, fpart, fpair, fhalf, fchip, fchunk, fsend, lowbuf, sqbuf, sqrecv, rightbuf,
@@ -419,39 +419,69 @@
             landed(buffer.at[:, pl.ds(pl.multiple_of(start, piece), piece), :], recv.at[j - 1])
         part = buffer.at[:, own, :]
         go(part, part, sent.at[chips - 1], recv.at[chips - 1], pair, z)
+    def present(c):
+        return sum(((owner[e] == z) & (position[e] == c)).astype(jnp.int32) for e in range(experts)) > 0
+
     for c in range(CAP):
         expert = taken(z, c)
         for k in range(kinds):
-            low_out[c * kinds + k, :urows] = obuf[(expert * kinds + k) * 2]
-            low_out[c * kinds + k, urows:] = obuf[(expert * kinds + k) * 2 + 1]
-
+            for h in range(2):
+                left = obuf[(expert * kinds + k) * 2 + h].astype(jnp.float32) * math.sqrt(D)
+                left_out[c * kinds + k, h * urows : (h + 1) * urows] = jnp.where(present(c), left, 0.0)
+
+    landed(lowbuf.at[:, theirs, :], low_recv.at[chips - 1])
     kept = []
 
     def keep(c, source, k):
+        m = c * kinds + k
         there = pl.ds(pl.multiple_of(source * columns, columns), columns)
-        copy = pltpu.make_async_copy(
-            place(c, source, k), got_out.at[c * kinds + k, :, there], out_sem.at[len(kept)]
-        )
+        expert = taken(z, c)
+        used = present(c)
+        for h in range(2):
+            @pl.loop(0, urows // 128)
+            def _(b):
+                at = pl.ds(pl.multiple_of(h * urows + b * 128, 128), 128)
+                low = obuf[(expert * kinds + k) * 2 + h, pl.ds(pl.multiple_of(b * 128, 128), 128), :]
+                update = jnp.dot(low, lowbuf[m, :, there], preferred_element_type=jnp.float32)
+                fresh = got[m, at, there].astype(jnp.float32) - feedback * update
+                got[m, at, there] = jnp.where(used, fresh, 0.0).astype(jnp.bfloat16)
+        copy = pltpu.make_async_copy(place(c, source, k), state_out.at[m, :, there], out_sem.at[len(kept)])
         copy.start()
         kept.append(copy)
 
-    for k in range(kinds):
-        keep(0, z, k)
-        keep(1, z, k)
+    for c in range(CAP):
+        for k in range(kinds):
+            keep(c, z, k)
+    landed(rightbuf.at[:, theirs, :], right_recv.at[chips - 1])
+    right_out[...] = rightbuf[...]
     for k in range(kinds):
         landed(place(1, near, k), near_recv.at[k])
         keep(1, near, k)
     for k in range(kinds):
-        for source in (near, far, far + 1):
-            landed(place(0, source, k), first_recv.at[source, k])
-            keep(0, source, k)
+        landed(place(0, near, k), first_recv.at[near, k])
+        keep(0, near, k)
+    for k in range(kinds):
+        for i in range(2):
+            landed(place(0, far + i, k), first_recv.at[far + i, k])
+            keep(0, far + i, k)
+
+        @pl.when(is_inner)
+        def _():
+            for i in range(2):
+                block = place(1, far + i, k)
+                remote(block, block, pass_send.at[i, k], pass_recv.at[i, k], f, near).wait_send()
+
+        @pl.when(is_outer)
+        def _():
+            for i in range(2):
+                landed(place(1, far + i, k), pass_recv.at[i, k])
+
+        for i in range(2):
+            keep(1, far + i, k)
 
     @pl.when(is_inner)
     def _():
         for i in range(2):
-            for k in range(kinds):
-                block = place(1, far + i, k)
-                remote(block, block, pass_send.at[i, k], pass_recv.at[i, k], f, near).wait_send()
             ortho_on(i).wait_send()
         for t, d in enumerate((outer, inner)):
             for i in range(units):
@@ -462,30 +492,11 @@
         for t, d in enumerate((outer, inner)):
             for i in range(units):
                 relay(t, i, d * units + i).wait_send()
-        for i in range(2):
-            for k in range(kinds):
-                landed(place(1, far + i, k), pass_recv.at[i, k])
-
-    for i in range(2):
-        for k in range(kinds):
-            keep(1, far + i, k)
-    for buffer, recv in ((lowbuf, low_recv), (rightbuf, right_recv)):
-        landed(buffer.at[:, theirs, :], recv.at[chips - 1])
-    fact_out[...] = lowbuf[...]
-    right_out[...] = rightbuf[...]
+
     for copy in started:
         copy.wait_send()
     for copy in kept:
         copy.wait()
-
-
-def fresh_kernel(used_ref, got_ref, low_ref, fact_ref, state_ref, left_ref):
-    m = pl.program_id(0)
-    update = jnp.dot(low_ref[0], fact_ref[0], preferred_element_type=jnp.float32)
-    fresh = got_ref[0].astype(jnp.float32) - feedback * update
-    state_ref[0] = jnp.where(used_ref[m] > 0, fresh, 0.0).astype(jnp.bfloat16)
-    left = low_ref[0].astype(jnp.float32) * math.sqrt(D)
-    left_ref[0] = jnp.where(used_ref[m] > 0, left, 0.0)
 
 
 def shards(momentum, gradient, right_in, owners):
@@ -495,15 +506,6 @@
     rank = right_in.shape[-1]
     hidden = groups * columns
     mats = CAP * kinds
-    z = lax.axis_index("tensor")
-    index_line = jnp.arange(experts, dtype=jnp.int32)
-    same_owner = owners[:, None] == owners[None, :]
-    earlier = index_line[None, :] < index_line[:, None]
-    position = jnp.sum((same_owner & earlier).astype(jnp.int32), axis=1)
-    slot = owners * CAP + position
-    here = slot[:, None] == (z * CAP + jnp.arange(mats, dtype=jnp.int32) // kinds)[None, :]
-    used = jnp.sum(here.astype(jnp.int32), axis=0)
-
     smem = pl.BlockSpec(memory_space=pltpu.SMEM)
     vmem = pl.BlockSpec(memory_space=pltpu.VMEM)
     hbm = pl.BlockSpec(memory_space=pl.ANY)
@@ -515,16 +517,15 @@
     units = 2 * every // groups
     piece = rank // shards_f
     near_z, near_c = groups - 1, chips - 1
-    got, low, fact, right = pl.pallas_call(
+    state, left, right = pl.pallas_call(
         functools.partial(step_kernel, shards_f, groups, kinds),
         out_shape=(
             shape((mats, rows, hidden), bf16),
-            shape((mats, rows, rank), bf16),
-            shape((mats, rank, hidden), bf16),
+            shape((mats, rows, rank), f32),
             shape((every, rank, columns), f32),
         ),
         in_specs=[smem, vmem, vmem, vmem],
-        out_specs=(hbm, vmem, vmem, vmem),
+        out_specs=(hbm, vmem, vmem),
         scratch_shapes=[
             pltpu.VMEM((every, rows, columns), bf16),
             pltpu.VMEM((5, kinds, rows, columns), bf16),
@@ -580,23 +581,6 @@
         right_in.reshape(every, columns, rank),
     )
 
-    band = min(rows, 256)
-    state, left = pl.pallas_call(
-        fresh_kernel,
-        grid=(mats, rows // band),
-        out_shape=(shape((mats, rows, hidden), bf16), shape((mats, rows, rank), f32)),
-        in_specs=[
-            smem,
-            pl.BlockSpec((1, band, hidden), lambda m, i: (m, i, 0)),
-            pl.BlockSpec((1, band, rank), lambda m, i: (m, i, 0)),
-            pl.BlockSpec((1, rank, hidden), lambda m, i: (m, 0, 0)),
-        ],
-        out_specs=(
-            pl.BlockSpec((1, band, hidden), lambda m, i: (m, i, 0)),
-            pl.BlockSpec((1, band, rank), lambda m, i: (m, i, 0)),
-        ),
-        name="fresh",
-    )(used, got, low, fact)
     right_new = jnp.swapaxes(right, 1, 2).reshape(experts, kinds, columns, rank)
     return (
         state.reshape(CAP, kinds, rows, hidden),

time: 183 us -> 182 us (level)
  local copies, waits for them, and re-layouts: 1.39 us -> 9.61 us
  Pallas kernels: 178 us -> 170 us
  other arithmetic: 2.17 us -> 0 us
    pallas_call x1 -> x0, Pallas kernels: 10.2 us -> none  [shards(): pl.pallas_call(fresh_kernel, grid=(mats, rows // band), out_shape=(shape(...]
    unnamed x3 -> x5, local copies, waits for them, and re-layouts: 1.39 us -> 9.61 us
    pallas_call x1, Pallas kernels: 168 us -> 170 us  [shards(): pl.pallas_call(functools.partial(step_kernel, shards_f, groups, kinds), o...]
where the time goes in v6:
time: 182 us; the launch traced here: 180 us
  Pallas kernels  170 us (93%)
  local copies, waits for them, and re-layouts  9.61 us (5%)
    pallas_call x1, Pallas kernels, shards(): pl.pallas_call(functools.partial(step_kernel, shards_f, groups, kinds), o...  170 us
    unnamed x5, local copies, waits for them, and re-layouts  9.61 us

profile of v6, /device:TPU:0, one launch (start us, length us, event | category | flops | bytes accessed | tf_op | source)
XLA Modules:
  0.0 180.4 jit_solution(5008705331403172543)
XLA Ops:
  0.6 170.2 %step.1 = (bf16[4,512,1536]{2,1,0:T(8,128)(2,1)}, f32[4,512,128]{2,1,0:T(8,128)}, f32[6,128,384]{2,1,0:T(8,128)}) custom-call(s32[3]{0:T(128)} %own_ref.1, bf16[6,512,384]{2,1,0:T(8,128)(2,1)} %bitcast.9, bf16[6,512,384]{2,1,0:T(8,128)(2,1)} %bitcast.10, bf16[6,384,128]{2,1,0:T(8,128)(2,1)} %bitcast.13), custom_call_target="tpu_custom_call" | custom-call | tf_op jit(solution)/shard_map/step/pallas_call | solution.py:520
  170.8 2.7 %copy.7 = f32[3,2,384,128]{3,2,1,0:T(8,128)} copy(f32[3,2,384,128]{2,3,1,0:T(8,128)} %bitcast.11) | data formatting | bytes 2359296
  173.4 0.0 copy-start
  173.5 6.0 %copy.10 = bf16[2,2,512,1536]{3,2,1,0:T(8,128)(2,1)} copy(bf16[2,2,512,1536]{3,2,1,0:T(8,128)(2,1)} %bitcast.8) | data formatting | bytes 12582912
  179.4 0.0 copy-done
  179.4 1.0 copy.11
Async XLA Ops:
  173.4 6.0 %copy-start = (f32[4,512,128]{2,1,0:T(8,128)S(1)}, f32[4,512,128]{2,1,0:T(8,128)}, u32[]{:S(2)}) copy-start(f32[4,512,128]{2,1,0:T(8,128)} %get-tuple-element.7) | copy-start | bytes 3145732

commit v7 on v6

--- a/solution.py
+++ b/solution.py
@@ -80,7 +80,7 @@
 
 MESH = pl.DeviceIdType.MESH
 HIGHEST = lax.Precision.HIGHEST
-VMEM_BYTES = 56 * 1024 * 1024
+VMEM_BYTES = 48 * 1024 * 1024
 
 
 def greet(shards_f, groups):
@@ -453,7 +453,8 @@
         for k in range(kinds):
             keep(c, z, k)
     landed(rightbuf.at[:, theirs, :], right_recv.at[chips - 1])
-    right_out[...] = rightbuf[...]
+    for m in range(mats):
+        right_out[m] = rightbuf[m].T
     for k in range(kinds):
         landed(place(1, near, k), near_recv.at[k])
         keep(1, near, k)
@@ -520,12 +521,12 @@
     state, left, right = pl.pallas_call(
         functools.partial(step_kernel, shards_f, groups, kinds),
         out_shape=(
-            shape((mats, rows, hidden), bf16),
-            shape((mats, rows, rank), f32),
-            shape((every, rank, columns), f32),
+            pltpu.VMEM((mats, rows, hidden), bf16),
+            pltpu.VMEM((mats, rows, rank), f32),
+            pltpu.VMEM((every, columns, rank), f32),
         ),
         in_specs=[smem, vmem, vmem, vmem],
-        out_specs=(hbm, vmem, vmem),
+        out_specs=(vmem, vmem, vmem),
         scratch_shapes=[
             pltpu.VMEM((every, rows, columns), bf16),
             pltpu.VMEM((5, kinds, rows, columns), bf16),
@@ -581,7 +582,7 @@
         right_in.reshape(every, columns, rank),
     )
 
-    right_new = jnp.swapaxes(right, 1, 2).reshape(experts, kinds, columns, rank)
+    right_new = right.reshape(experts, kinds, columns, rank)
     return (
         state.reshape(CAP, kinds, rows, hidden),
         left.reshape(CAP, kinds, rows, rank),

time: 182 us -> 176 us (0.967)
  local copies, waits for them, and re-layouts: 9.61 us -> 4.69 us
    unnamed x5 -> x3, local copies, waits for them, and re-layouts: 9.61 us -> 4.69 us
where the time goes in v7:
time: 176 us; the launch traced here: 174 us
  Pallas kernels  169 us (96%)
  local copies, waits for them, and re-layouts  4.69 us (3%)
    pallas_call x1, Pallas kernels, shards(): pl.pallas_call(functools.partial(step_kernel, shards_f, groups, kinds), o...  169 us
    unnamed x3, local copies, waits for them, and re-layouts  4.69 us

profile of v7, /device:TPU:0, one launch (start us, length us, event | category | flops | bytes accessed | tf_op | source)
XLA Modules:
  0.0 174.4 jit_solution(2097199261707423714)
XLA Ops:
  0.6 169.1 %step.1 = (bf16[4,512,1536]{2,1,0:T(8,128)(2,1)S(1)}, f32[4,512,128]{2,1,0:T(8,128)S(1)}, f32[6,384,128]{2,1,0:T(8,128)S(1)}) custom-call(s32[3]{0:T(128)} %own_ref.1, bf16[6,512,384]{2,1,0:T(8,128)(2,1)} %bitcast.9, bf16[6,512,384]{2,1,0:T(8,128)(2,1)} %bitcast.10, bf16[6,384,128]{2,1,0:T(8,128)(2,1)} %bitcast.11), custom_call_target="tpu_custom_call" | custom-call | tf_op jit(solution)/shard_map/step/pallas_call | solution.py:521
  169.7 2.7 %copy.10 = bf16[2,2,512,1536]{3,2,1,0:T(8,128)(2,1)} copy(bf16[2,2,512,1536]{3,2,1,0:T(8,128)(2,1)S(1)} %bitcast.6) | data formatting | bytes 12582912
  172.5 1.0 copy.11
  173.4 1.0 copy.12

commit v8 on v7

--- a/solution.py
+++ b/solution.py
@@ -290,13 +290,6 @@
     gram[0] = gram_of(odd) + gram_of(odd + 1)
     shared.wait_recv()
     gram[1] = gram[2] + gnear[...]
-    far_second(0)
-    near_second(0)
-    far_second(1)
-    near_second(1)
-    near_first(0)
-    near_first(1)
-    far_outer(0)
     go(gram.at[1 - core], gpair, ga_send.at[1], ga_recv.at[1], pair, z).wait_recv()
     total = gram[core] + gpair[...]
     ghalf[...] = total
@@ -305,6 +298,13 @@
             ghalf, gchip.at[j - 1], gb_send.at[j - 1], gb_recv.at[j - 1],
             lax.rem(chip + j, chips) * 2 + core, z,
         )
+    far_second(0)
+    near_second(0)
+    far_second(1)
+    near_second(1)
+    near_first(0)
+    near_first(1)
+    far_outer(0)
     for j in range(1, chips):
         landed(gchip.at[j - 1], gb_recv.at[j - 1])
         total = total + gchip[j - 1]
@@ -344,9 +344,6 @@
     def _():
         for i in range(2):
             landed(chunk_of(far + i), op_recv.at[i])
-
-    far_inner(0)
-    hand_on(0)
 
     for m in range(mats):
         fpart[m] = jnp.dot(
@@ -369,6 +366,8 @@
             fchip.at[j - 1], fb_send.at[j - 1], fb_recv.at[j - 1], other * 2 + core, z,
         )
     total = fhalf[:, pl.ds(pl.multiple_of(chip * piece, piece), piece), :]
+    far_inner(0)
+    hand_on(0)
     for j in range(1, chips):
         landed(fchip.at[j - 1], fb_recv.at[j - 1])
         total = total + fchip[j - 1]

time: 176 us -> 191 us (1.085)
  Pallas kernels: 169 us -> 186 us
    pallas_call x1, Pallas kernels: 169 us -> 186 us  [shards(): pl.pallas_call(functools.partial(step_kernel, shards_f, groups, kinds), o...]
where the time goes in v8:
time: 191 us
  Pallas kernels  186 us (97%)
  local copies, waits for them, and re-layouts  4.69 us (2%)
    pallas_call x1, Pallas kernels, shards(): pl.pallas_call(functools.partial(step_kernel, shards_f, groups, kinds), o...  186 us
    unnamed x3, local copies, waits for them, and re-layouts  4.69 us

profile of v8, /device:TPU:0, one launch (start us, length us, event | category | flops | bytes accessed | tf_op | source)
XLA Modules:
  0.0 190.9 jit_solution(4631187698343569851)
XLA Ops:
  0.6 185.6 %step.1 = (bf16[4,512,1536]{2,1,0:T(8,128)(2,1)S(1)}, f32[4,512,128]{2,1,0:T(8,128)S(1)}, f32[6,384,128]{2,1,0:T(8,128)S(1)}) custom-call(s32[3]{0:T(128)} %own_ref.1, bf16[6,512,384]{2,1,0:T(8,128)(2,1)} %bitcast.9, bf16[6,512,384]{2,1,0:T(8,128)(2,1)} %bitcast.10, bf16[6,384,128]{2,1,0:T(8,128)(2,1)} %bitcast.11), custom_call_target="tpu_custom_call" | custom-call | tf_op jit(solution)/shard_map/step/pallas_call | solution.py:520
  186.2 2.7 %copy.10 = bf16[2,2,512,1536]{3,2,1,0:T(8,128)(2,1)} copy(bf16[2,2,512,1536]{3,2,1,0:T(8,128)(2,1)S(1)} %bitcast.6) | data formatting | bytes 12582912
  188.9 1.0 copy.11
  189.9 1.0 copy.12
